TPU v7x, 32 devices: a whole 2x2x4 slice. The times are simulated.
32 devices in a mesh: chan: 16 (over z, x, core), tm: 2 (over y).
Axes of the slice: x: 2, y: 2, z: 4, core: 2. Of those that a mesh axis runs over, the one named last changes fastest.
Arguments:
- spectra: bfloat16 [16, 512, 2, 2048], P('tm', 'chan'), may hold values from -74 to 74
- src_block: int32 [2], replicated, may hold values from 0 to 15
- quality: int32 [512], P('chan'), may hold values 0 or 1
Outputs:
- stacked: float32 [32, 2, 512, 512], P('tm', None, 'chan')
All inputs are finite; a program needn't handle non-finite values. No bound on the sum of `quality` on one device may be relied on, other than what follows from the above.
Results may differ from a plain program's by a relative error of at most 0.0054.
Values may be sent and summed in bfloat16 or wider, within the bound.
No kernel may reach another device: no remote copies, remote signals or barrier semaphores. Data moves between devices by JAX's collectives and lax.ppermute only.
A program may use at most 64 MiB of HBM per device.

v0:
```python
from functools import partial
import math

import jax
import jax.numpy as jnp
import numpy as np
from jax import lax
from jax.experimental import pallas as pl
from jax.experimental.pallas import tpu as pltpu
from jax.sharding import PartitionSpec as P

LAG = 512
STEPS = 2
LANES = 128
PACK = 16
BLOCKS = 8


def lag_table(num_bins, num_lags, windows):
    freq_bins = np.arange(num_bins, dtype=np.int64)[:, None]
    shifts = np.arange(num_lags, dtype=np.int64)[None, :] - num_lags // 2
    phases = np.mod(freq_bins * shifts, 2 * num_bins).astype(np.float32) * np.float32(
        math.pi / num_bins
    )
    scaling = np.float32(1.0 / math.sqrt(2.0 * num_bins * windows))
    table = np.concatenate([np.cos(phases) * scaling, -np.sin(phases) * scaling], 0)
    return jnp.asarray(table.astype(jnp.bfloat16))


def cross_kernel(place, *refs):
    *pieces, rcv_ref, cross_ref, src = refs
    blocks, windows, _, sources, bins = pieces[0].shape
    channels = rcv_ref.shape[2]
    num_bins = rcv_ref.shape[3]
    order = place[0]
    groups = range(0, channels, PACK)

    def widen(w, carry):
        for at, ref in enumerate(pieces):
            for entry in range(blocks):
                for part in range(2):
                    value = ref[entry, w, part].astype(jnp.float32)
                    for low in range(0, sources, 8):
                        src[at * blocks + entry, low // 8, 2 * w + part] = value[low : low + 8]
        return carry

    lax.fori_loop(0, windows, widen, 0)

    def lane_group(entry, lane):
        here = pl.multiple_of((entry ^ order) * bins + lane, LANES)
        there = pl.multiple_of(num_bins + here, LANES)
        lanes = pl.ds(lane, LANES)
        received = [
            [
                [rcv_ref[w, part, pl.ds(chan, PACK), pl.ds(here, LANES)] for chan in groups]
                for part in range(2)
            ]
            for w in range(windows)
        ]
        for s in range(sources):

            def summed(first, last):
                if last - first > 1:
                    middle = (first + last) // 2
                    left, right = summed(first, middle), summed(middle, last)
                    return [a + b for a, b in zip(left, right)]
                s_re, s_im = [
                    jnp.broadcast_to(
                        src[entry, s // 8, 2 * first + part, pl.ds(s % 8, 1), lanes], (PACK, LANES)
                    ).astype(jnp.bfloat16)
                    for part in range(2)
                ]
                values = []
                for c_re, c_im in zip(*received[first]):
                    values.append(s_re * c_re + s_im * c_im)
                    values.append(s_re * c_im - s_im * c_re)
                return values

            values = summed(0, windows)
            for g, chan in enumerate(groups):
                rows = pl.ds(chan, PACK)
                cross_ref[s, rows, pl.ds(here, LANES)] = values[2 * g]
                cross_ref[s, rows, pl.ds(there, LANES)] = values[2 * g + 1]

    def body(entry, carry):
        for lane in range(0, bins, LANES):
            lane_group(entry, lane)
        return carry

    lax.fori_loop(0, len(pieces) * blocks, body, 0)


@jax.jit
def cross_spectra(order, pieces, receivers):
    blocks, windows, _, sources, bins = pieces[0].shape
    channels, num_bins = receivers.shape[2:]
    vmem = pl.BlockSpec(memory_space=pltpu.VMEM)
    return pl.pallas_call(
        cross_kernel,
        in_specs=[pl.BlockSpec(memory_space=pltpu.SMEM)] + [vmem] * (len(pieces) + 1),
        out_specs=vmem,
        scratch_shapes=[
            pltpu.VMEM((len(pieces) * blocks, sources // 8, 2 * windows, 8, bins), jnp.float32)
        ],
        out_shape=jax.ShapeDtypeStruct((sources, channels, 2 * num_bins), jnp.bfloat16),
        compiler_params=pltpu.CompilerParams(vmem_limit_bytes=8 * 1024 * 1024),
        cost_estimate=pl.CostEstimate(
            flops=sources * channels * num_bins * windows * 8,
            bytes_accessed=sources * channels * num_bins,
            transcendentals=0,
        ),
    )(order[None], *pieces, receivers)


def after(value, *others):
    return lax.optimization_barrier((value,) + others)[0]


def per_device(spectra, src_block, quality):
    windows, channels, _, num_bins = spectra.shape
    tm = lax.axis_size("tm")
    chan = lax.axis_size("chan")
    me = lax.axis_index("chan")
    my_tm = lax.axis_index("tm")
    kept = channels // tm
    bit = lambda value, place: (value >> place) & 1
    swap = lambda value, place: lax.ppermute(
        value, "chan", [(i, i ^ (1 << place)) for i in range(chan)]
    )

    def cut(value, axis, start, size):
        at = [0] * value.ndim
        at[axis] = start
        sizes = list(value.shape)
        sizes[axis] = size
        return lax.dynamic_slice(value, at, sizes, allow_negative_indices=False)

    raw = lax.optimization_barrier(spectra.transpose(0, 2, 1, 3))
    half = num_bins // 2
    own_half = (me & 1) * half
    mine = cut(raw, 3, own_half, half)
    given = swap(cut(raw, 3, half - own_half, half), 0)
    usable = quality.astype(jnp.float32)[None, :]
    wide = raw.astype(jnp.float32)
    power = jnp.mean(wide * wide, axis=(1, 3)) * usable
    scale = usable / jnp.sqrt(power + 1e-06)
    given_scale = swap(scale, 0)
    receivers = (wide * scale[:, None, :, None]).astype(jnp.bfloat16)
    table = lag_table(num_bins, LAG, windows * tm)

    steps = range(STEPS)
    apart = [src_block[step] ^ me for step in steps]

    def starts_of(size):
        out = []
        for place in (1, 2):
            own = (me & (1 << place)) * (size >> place)
            out.append([own, size - own])
        return out

    def same_side(place):
        return [(apart[step] & (1 << place)) == 0 for step in steps]

    first_rows = [(1 - my_tm) * kept, my_tm * kept]
    given_scale, *early = lax.optimization_barrier(
        (given_scale, same_side(0), starts_of(half // 2), first_rows)
    )
    same, starts, first_rows = {0: early[0]}, {half // 2: early[1]}, early[2]

    def later_scalars(value):
        late = ([same_side(place) for place in (1, 2, 3)], starts_of(half // 4))
        value, (sides, starts[half // 4]) = lax.optimization_barrier((value, late))
        same.update(zip((1, 2, 3), sides))
        return value

    def part_of(value, place, other):
        size = value.shape[-1] // 2
        return cut(value, value.ndim - 1, starts[size][place - 1][other], size)

    def chosen(step, part, place, other):
        here = same[0][step]
        factor = jnp.where(here, scale, given_scale)
        value = jnp.where(here, part_of(mine, place, other), part_of(given, place, other))
        value = value.astype(jnp.float32) * factor[:, None, :, None]
        value = cut(value.astype(jnp.bfloat16), 2, first_rows[part], kept)
        if chan > 16:
            groups = [list(range(i, chan, 16)) for i in range(16)]
            value = jnp.where(src_block[step] // 16 == me // 16, value, 0)
            value = lax.psum(value, "chan", axis_index_groups=groups)
        return value

    places = [(1, 2) if step % 2 == 0 else (2, 1) for step in steps]

    def broadcast(part, ahead=None):
        tie = lambda value, phase: after(value, *ahead[max(phase, 1)]) if ahead else value
        seen = []
        have = []
        for step in steps:
            first = places[step][0]
            have.append(tie(chosen(step, part, first, 1), 0))
        have = [
            swap(value, places[step][0])
            for step, value in zip(steps, lax.optimization_barrier(tuple(have)))
        ]
        if not ahead:
            have = later_scalars(have)
        seen.append(tuple(have))
        for step in steps:
            first = places[step][0]
            have[step] = jnp.where(same[first][step], chosen(step, part, first, 0), have[step])
        come = []
        for step in steps:
            second = places[step][1]
            come.append(swap(tie(part_of(have[step], second, 1), 1), second))
        seen.append(tuple(come))
        for step in steps:
            second = places[step][1]
            own = part_of(have[step], second, 0)
            have[step] = jnp.where(same[second][step], own, come[step])
        stacked = tie(jnp.stack(have), 2)
        come = swap(stacked, 3)
        seen.append((come,))
        work = yield stacked
        come = after(come, *work[0])
        for step in steps:
            have[step] = jnp.where(same[3][step], have[step], come[step])[None]
        come = [swap(tie(have[step], 3), places[step][1]) for step in steps]
        seen.append(tuple(come))
        come = [after(value, *come, *work[1]) for value in come]
        have = [jnp.concatenate(pair, 0) for pair in zip(have, come)]
        come = [swap(tie(have[step], 4), places[step][0]) for step in steps]
        seen.append(tuple(come))
        yield have, come, seen

    def whole(have, come, behind, joined=False):
        come = after(come, *behind)
        pieces = [jnp.concatenate([have, come], 0)] if joined else [have, come]
        return pieces + [swap(piece, 0) for piece in pieces]

    def lags(cross):
        return jnp.dot(
            cross.reshape(kept * channels, 2 * num_bins),
            table,
            preferred_element_type=jnp.float32,
        )

    orders = [
        bit(me, 0) * 4 + bit(me, first) * 2 + bit(me, second) for first, second in places
    ]
    partners = [(i, i ^ 1) for i in range(tm)]
    send = broadcast(0)
    next(send)
    have, more, seen = send.send(((), ()))
    keep = broadcast(1, seen)
    work = []
    sent = []
    operand = next(keep)
    behind = []
    for step in steps:
        first, *rest = whole(have[step], more[step], behind, not step)
        work.append(cross_spectra(orders[step], (after(first, *sent), *rest), receivers))
        sent.append(lags(work[step]).astype(jnp.bfloat16))
        behind = work[:1]
    have, more, _ = keep.send((work[:1], sent[:1]))
    come = [lax.ppermute(value, "tm", partners) for value in sent]
    cross = []
    for step in steps:
        first, *rest = whole(have[step], more[step], work[1:])
        first = after(first, *sent, *cross, *come[:step])
        cross.append(cross_spectra(orders[step], (first, *rest), receivers))
    come = [after(value, cross[-1]) for value in come]
    outs = [lags(after(value, *come)) for value in cross]
    outs = lax.optimization_barrier(outs)
    outs = [
        (out + got.astype(jnp.float32)).reshape(kept, channels, LAG)
        for out, got in zip(outs, come)
    ]
    return jnp.stack(outs, 1)


def solution(mesh):
    return jax.shard_map(
        per_device,
        mesh=mesh,
        in_specs=(P("tm", "chan", None, None), P(), P("chan")),
        out_specs=P("tm", None, "chan", None),
        check_vma=False,
    )
```

profile of v0, /device:TPU:0, one launch (start us, length us, event | category | flops | bytes accessed | tf_op | source)
XLA Modules:
  0.0 105.8 jit_solution(8554117913726376313)
XLA Ops:
  0.0 2.5 %copy.9 = bf16[8,32,2,2048]{3,1,2,0:T(8,128)(2,1)S(1)} copy(bf16[8,32,2,2048]{3,2,1,0:T(2,128)(2,1)} %param.4) | data formatting | bytes 4194304 | tf_op args[0]
  2.5 1.2 %constant_dynamic-slice_fusion.8 = bf16[8,2,32,1024]{3,2,1,0:T(8,128)(2,1)} fusion(bf16[8,2,32,2048]{3,2,1,0:T(8,128)(2,1)S(1)} %bitcast.65, s32[]{:T(128)S(6)} %sub.21), kind=kLoop, calls=%fused_computation.51 | loop fusion | bytes 2097156 | tf_op jit(solution)/shard_map/dynamic_slice | solution.py:136
  4.8 0.7 fusion.12
  6.8 4.1 %multiply_convert_fusion = (bf16[8,2,32,512]{3,2,1,0:T(8,128)(2,1)}, bf16[8,2,32,512]{3,2,1,0:T(8,128)(2,1)S(1)}, bf16[8,2,32,512]{3,2,1,0:T(8,128)(2,1)S(1)}, bf16[8,2,32,512]{3,2,1,0:T(8,128)(2,1)}) fusion(bf16[8,2,32,1024]{3,2,1,0:T(8,128)(2,1)S(1)} %collective-permute-done.1, s32[]{:T(128)S(6)} %mul.112, bf16[8,2,32,2048]{3,2,1,0:T(8,128)(2,1)S(1)} %bitcast.67, ...), kind=kLoop, calls=%fused_computation.10 | loop fusion | flops 4194304 | bytes 6293538 | tf_op jit(solution)/shard_map/convert_element_type | solution.py:185
  11.4 3.0 %collective-permute-start.2 = (bf16[8,2,16,512]{3,2,1,0:T(8,128)(2,1)S(1)}, bf16[8,2,16,512]{3,2,1,0:T(8,128)(2,1)S(1)}, u32[]{:S(2)}, u32[]{:S(2)}) collective-permute-start(bf16[8,2,16,512]{3,2,1,0:T(8,128)(2,1)S(1)} %get-tuple-element.62), channel_id=1, source_target_pairs={{0,4},{2,6},{4,0},{6,2},{8,12},{10,14},{12,8},{14,10},{16,20},{18,... | collective-permute-start | bytes 786440 | tf_op jit(solution)/shard_map/ppermute | solution.py:127
  14.4 1.6 %collective-permute-start.3 = (bf16[8,2,16,512]{3,2,1,0:T(8,128)(2,1)S(1)}, bf16[8,2,16,512]{3,2,1,0:T(8,128)(2,1)S(1)}, u32[]{:S(2)}, u32[]{:S(2)}) collective-permute-start(bf16[8,2,16,512]{3,2,1,0:T(8,128)(2,1)S(1)} %get-tuple-element.63), channel_id=1, source_target_pairs={{0,8},{2,10},{4,12},{6,14},{8,0},{10,2},{12,4},{14,6},{16,24},{18,... | collective-permute-start | bytes 786440 | tf_op jit(solution)/shard_map/ppermute | solution.py:127
  16.0 4.9 %collective-permute-done.2 = bf16[8,2,16,512]{3,2,1,0:T(8,128)(2,1)S(1)} collective-permute-done((bf16[8,2,16,512]{3,2,1,0:T(8,128)(2,1)S(1)}, bf16[8,2,16,512]{3,2,1,0:T(8,128)(2,1)S(1)}, u32[]{:S(2)}, u32[]{:S(2)}) %collective-permute-start.2) | collective-permute-done | bytes 262176 | tf_op jit(solution)/shard_map/ppermute | solution.py:127
  20.9 1.5 %collective-permute-done.3 = bf16[8,2,16,512]{3,2,1,0:T(8,128)(2,1)S(1)} collective-permute-done((bf16[8,2,16,512]{3,2,1,0:T(8,128)(2,1)S(1)}, bf16[8,2,16,512]{3,2,1,0:T(8,128)(2,1)S(1)}, u32[]{:S(2)}, u32[]{:S(2)}) %collective-permute-start.3) | collective-permute-done | bytes 262176 | tf_op jit(solution)/shard_map/ppermute | solution.py:127
  22.4 1.1 %dynamic-slice_select_fusion.2 = bf16[8,2,16,512]{3,2,1,0:T(8,128)(2,1)S(1)} fusion(bf16[8,2,16,512]{3,2,1,0:T(8,128)(2,1)S(1)} %collective-permute-done.2, bf16[8,2,32,512]{3,2,1,0:T(8,128)(2,1)} %get-tuple-element.112, s32[]{:T(128)S(6)} %mul.113, pred[]{:T(512)S(6)} %eq.26), kind=kLoop, calls=%fused_computation.23 | loop fusion | flops 131072 | bytes 786437 | tf_op jit(solution)/shard_map/jit(_where)/select_n | solution.py:210
  23.6 1.6 %collective-permute-start.4 = (bf16[8,2,16,256]{3,2,1,0:T(8,128)(2,1)S(1)}, bf16[8,2,16,256]{3,2,1,0:T(8,128)(2,1)S(1)}, u32[]{:S(2)}, u32[]{:S(2)}) collective-permute-start(bf16[8,2,16,256]{3,2,1,0:T(8,128)(2,1)S(1)} %constant_dynamic-slice_fusion.3), channel_id=1, source_target_pairs={{0,8},{2,10},{4,12},{6,14},{8,0},{10,2},{12,4},{14,6},{16,24},{18,... | collective-permute-start | bytes 393224 | tf_op jit(solution)/shard_map/ppermute | solution.py:127
  25.2 1.1 %dynamic-slice_select_fusion.1 = bf16[8,2,16,512]{3,2,1,0:T(8,128)(2,1)S(1)} fusion(bf16[8,2,16,512]{3,2,1,0:T(8,128)(2,1)S(1)} %collective-permute-done.3, bf16[8,2,32,512]{3,2,1,0:T(8,128)(2,1)} %get-tuple-element.107, s32[]{:T(128)S(6)} %mul.113, pred[]{:T(512)S(6)} %eq.29), kind=kLoop, calls=%fused_computation.22 | loop fusion | flops 131072 | bytes 786437 | tf_op jit(solution)/shard_map/jit(_where)/select_n | solution.py:210
  26.4 0.6 collective-permute-start.5
  27.0 1.6 %collective-permute-done.4 = bf16[8,2,16,256]{3,2,1,0:T(8,128)(2,1)S(1)} collective-permute-done((bf16[8,2,16,256]{3,2,1,0:T(8,128)(2,1)S(1)}, bf16[8,2,16,256]{3,2,1,0:T(8,128)(2,1)S(1)}, u32[]{:S(2)}, u32[]{:S(2)}) %collective-permute-start.4) | collective-permute-done | bytes 131104 | tf_op jit(solution)/shard_map/ppermute | solution.py:127
  28.7 2.7 %collective-permute-done.5 = bf16[8,2,16,256]{3,2,1,0:T(8,128)(2,1)S(1)} collective-permute-done((bf16[8,2,16,256]{3,2,1,0:T(8,128)(2,1)S(1)}, bf16[8,2,16,256]{3,2,1,0:T(8,128)(2,1)S(1)}, u32[]{:S(2)}, u32[]{:S(2)}) %collective-permute-start.5) | collective-permute-done | bytes 131104 | tf_op jit(solution)/shard_map/ppermute | solution.py:127
  31.6 2.7 %collective-permute-start.10 = (bf16[2,8,2,16,256]{4,3,2,1,0:T(8,128)(2,1)S(1)}, bf16[2,8,2,16,256]{4,3,2,1,0:T(8,128)(2,1)S(1)}, u32[]{:S(2)}, u32[]{:S(2)}) collective-permute-start(bf16[2,8,2,16,256]{4,3,2,1,0:T(8,128)(2,1)S(1)} %pad_maximum_fusion.3), channel_id=1, source_target_pairs={{0,16},{2,18},{4,20},{6,22},{8,24},{10,26},{12,28},{14,30},{16,0},... | collective-permute-start | bytes 786440 | tf_op jit(solution)/shard_map/ppermute | solution.py:127
  34.2 0.5 collective-permute-start.6
  35.2 8.7 %collective-permute-done.10 = bf16[2,8,2,16,256]{4,3,2,1,0:T(8,128)(2,1)S(1)} collective-permute-done((bf16[2,8,2,16,256]{4,3,2,1,0:T(8,128)(2,1)S(1)}, bf16[2,8,2,16,256]{4,3,2,1,0:T(8,128)(2,1)S(1)}, u32[]{:S(2)}, u32[]{:S(2)}) %collective-permute-start.10) | collective-permute-done | bytes 262176 | tf_op jit(solution)/shard_map/ppermute | solution.py:127
  44.2 0.6 collective-permute-start.13
  45.1 2.1 %collective-permute-start.7 = (bf16[8,2,16,256]{3,2,1,0:T(8,128)(2,1)S(1)}, bf16[8,2,16,256]{3,2,1,0:T(8,128)(2,1)S(1)}, u32[]{:S(2)}, u32[]{:S(2)}) collective-permute-start(bf16[8,2,16,256]{3,2,1,0:T(8,128)(2,1)S(1)} %constant_dynamic-slice_fusion), channel_id=1, source_target_pairs={{0,8},{2,10},{4,12},{6,14},{8,0},{10,2},{12,4},{14,6},{16,24},{18,... | collective-permute-start | bytes 393224 | tf_op jit(solution)/shard_map/ppermute | solution.py:127
  47.4 1.5 %collective-permute-start.9 = (bf16[8,2,16,256]{3,2,1,0:T(8,128)(2,1)S(1)}, bf16[8,2,16,256]{3,2,1,0:T(8,128)(2,1)S(1)}, u32[]{:S(2)}, u32[]{:S(2)}) collective-permute-start(bf16[8,2,16,256]{3,2,1,0:T(8,128)(2,1)S(1)} %constant_dynamic-slice_fusion.6), channel_id=1, source_target_pairs={{0,4},{2,6},{4,0},{6,2},{8,12},{10,14},{12,8},{14,10},{16,20},{18,... | collective-permute-start | bytes 393224 | tf_op jit(solution)/shard_map/ppermute | solution.py:127
  49.0 0.8 collective-permute-done.13
  49.8 1.0 collective-permute-done.12
  50.8 1.4 %collective-permute-start.14 = (bf16[2,8,2,16,256]{4,3,2,1,0:T(8,128)(2,1)S(1)}, bf16[2,8,2,16,256]{4,3,2,1,0:T(8,128)(2,1)S(1)}, u32[]{:S(2)}, u32[]{:S(2)}) collective-permute-start(bf16[2,8,2,16,256]{4,3,2,1,0:T(8,128)(2,1)S(1)} %pad_maximum_fusion.4), channel_id=1, source_target_pairs={{0,4},{2,6},{4,0},{6,2},{8,12},{10,14},{12,8},{14,10},{16,20},{18,... | collective-permute-start | bytes 786440 | tf_op jit(solution)/shard_map/ppermute | solution.py:127
  52.2 0.5 collective-permute-start.18
  52.9 1.0 collective-permute-done.9
  54.0 0.7 pad_maximum_fusion.2
  54.7 1.7 %collective-permute-start.11 = (bf16[2,8,2,16,256]{4,3,2,1,0:T(8,128)(2,1)}, bf16[2,8,2,16,256]{4,3,2,1,0:T(8,128)(2,1)}, u32[]{:S(2)}, u32[]{:S(2)}) collective-permute-start(bf16[2,8,2,16,256]{4,3,2,1,0:T(8,128)(2,1)} %pad_maximum_fusion.2), channel_id=1, source_target_pairs={{0,16},{2,18},{4,20},{6,22},{8,24},{10,26},{12,28},{14,30},{16,0},... | collective-permute-start | bytes 786440 | tf_op jit(solution)/shard_map/ppermute | solution.py:127
  56.4 1.4 %collective-permute-done.14 = bf16[2,8,2,16,256]{4,3,2,1,0:T(8,128)(2,1)S(1)} collective-permute-done((bf16[2,8,2,16,256]{4,3,2,1,0:T(8,128)(2,1)S(1)}, bf16[2,8,2,16,256]{4,3,2,1,0:T(8,128)(2,1)S(1)}, u32[]{:S(2)}, u32[]{:S(2)}) %collective-permute-start.14) | collective-permute-done | bytes 262176 | tf_op jit(solution)/shard_map/ppermute | solution.py:127
  58.0 0.7 fusion.1.refs_2_.refs_4_
  58.7 0.6 collective-permute-start.19
  59.2 0.6 collective-permute-done.15.refs_1_
  59.9 5.6 %cross_spectra.4 = bf16[16,32,4096]{2,1,0:T(8,128)(2,1)S(1)} custom-call(s32[1]{0:T(128)} %bitcast.place, bf16[4,8,2,16,256]{4,3,2,1,0:T(8,128)(2,1)S(1)} %pad_maximum_fusion.1.refs_0_, bf16[4,8,2,16,256]{4,3,2,1,0:T(8,128)(2,1)S(1)} %collective-permute-done.15.refs_1_, bf16[8,2,32,2048]{3,2,1,0:T(8,128)(2,1)S(1)} %fusion.1.refs_2_.refs_4_), custom_call_target="tpu_custom_call" | custom-call | flops 67108864 | bytes 1048576 | tf_op jit(solution)/shard_map/jit(cross_spectra)/pallas_call | solution.py:98
  65.4 1.2 %collective-permute-done.11 = bf16[2,8,2,16,256]{4,3,2,1,0:T(8,128)(2,1)} collective-permute-done((bf16[2,8,2,16,256]{4,3,2,1,0:T(8,128)(2,1)}, bf16[2,8,2,16,256]{4,3,2,1,0:T(8,128)(2,1)}, u32[]{:S(2)}, u32[]{:S(2)}) %collective-permute-start.11) | collective-permute-done | bytes 262176 | tf_op jit(solution)/shard_map/ppermute | solution.py:127
  66.6 1.2 %fusion.6 = (bf16[1,8,2,16,256]{4,3,2,1,0:T(8,128)(2,1)S(1)}, bf16[1,8,2,16,256]{4,3,2,1,0:T(8,128)(2,1)S(1)}) fusion(bf16[2,8,2,16,256]{4,3,2,1,0:T(8,128)(2,1)} %collective-permute-done.11, pred[]{:T(512)S(6)} %eq.31, bf16[8,2,16,256]{3,2,1,0:T(8,128)(2,1)S(1)} %copy-done.9, bf16[8,2,16,512]{3,2,1,0:T(8,128)(2,1)S(1)} %copy-done.7, s32[]{:T(128)S(6)} %mul.121, ...), kind=kLoop, calls=%fused_computation.32 | loop fusion | flops 262144 | bytes 1048588 | tf_op jit(solution)/shard_map/broadcast_in_dim | solution.py:226
  67.9 1.0 collective-permute-start.17
  69.0 2.3 %convolution_convert_fusion.1 = bf16[512,512]{1,0:T(8,128)(2,1)S(1)} fusion(bf16[512,4096]{1,0:T(8,128)(2,1)S(1)} %bitcast.61, bf16[4096,512]{1,0:T(8,128)(2,1)S(1)} %copy-done.12), kind=kOutput, calls=%fused_computation.7 | convolution fusion | flops 2147745792 | bytes 8912896 | tf_op jit(solution)/shard_map/dot_general | solution.py:241
  71.3 1.7 %collective-permute-start.24 = (bf16[512,512]{1,0:T(8,128)(2,1)S(1)}, bf16[512,512]{1,0:T(8,128)(2,1)S(1)}, u32[]{:S(2)}, u32[]{:S(2)}) collective-permute-start(bf16[512,512]{1,0:T(8,128)(2,1)S(1)} %convolution_convert_fusion.1), channel_id=1, source_target_pairs={{0,1},{1,0},{2,3},{3,2},{4,5},{5,4},{6,7},{7,6},{8,9},{9,8},{10,11... | collective-permute-start | bytes 1572872 | tf_op jit(solution)/shard_map/ppermute | solution.py:265
  73.3 2.0 %collective-permute-start.25 = (bf16[2,8,2,16,256]{4,3,2,1,0:T(8,128)(2,1)S(1)}, bf16[2,8,2,16,256]{4,3,2,1,0:T(8,128)(2,1)S(1)}, u32[]{:S(2)}, u32[]{:S(2)}) collective-permute-start(bf16[2,8,2,16,256]{4,3,2,1,0:T(8,128)(2,1)S(1)} %pad_maximum_fusion.7.refs_0_), channel_id=1, source_target_pairs={{0,8},{2,10},{4,12},{6,14},{8,0},{10,2},{12,4},{14,6},{16,24},{18,... | collective-permute-start | bytes 786440 | tf_op jit(solution)/shard_map/ppermute | solution.py:127
  75.3 1.1 %collective-permute-start.21 = (bf16[2,8,2,16,256]{4,3,2,1,0:T(8,128)(2,1)S(1)}, bf16[2,8,2,16,256]{4,3,2,1,0:T(8,128)(2,1)S(1)}, u32[]{:S(2)}, u32[]{:S(2)}) collective-permute-start(bf16[2,8,2,16,256]{4,3,2,1,0:T(8,128)(2,1)S(1)} %pad_maximum_fusion.5.refs_0_), channel_id=1, source_target_pairs={{0,4},{2,6},{4,0},{6,2},{8,12},{10,14},{12,8},{14,10},{16,20},{18,... | collective-permute-start | bytes 786440 | tf_op jit(solution)/shard_map/ppermute | solution.py:127
  76.4 6.5 %cross_spectra.5 = bf16[16,32,4096]{2,1,0:T(8,128)(2,1)S(1)} custom-call(s32[1]{0:T(128)} %bitcast.17.place, bf16[2,8,2,16,256]{4,3,2,1,0:T(8,128)(2,1)S(1)} %pad_maximum_fusion.6.refs_0_, bf16[2,8,2,16,256]{4,3,2,1,0:T(8,128)(2,1)} %collective-permute-done.18.refs_1_, bf16[2,8,2,16,256]{4,3,2,1,0:T(8,128)(2,1)S(1)} %collective-permute-done.19.refs_2_, ...), custom_call_target="tpu_custom_call" | custom-call | flops 67108864 | bytes 1048576 | tf_op jit(solution)/shard_map/jit(cross_spectra)/pallas_call | solution.py:98
  82.9 2.3 %convolution_convert_fusion = bf16[512,512]{1,0:T(8,128)(2,1)S(1)} fusion(bf16[512,4096]{1,0:T(8,128)(2,1)S(1)} %bitcast.64, bf16[4096,512]{1,0:T(8,128)(2,1)S(1)} %copy-done.12), kind=kOutput, calls=%fused_computation.6 | convolution fusion | flops 2147745792 | bytes 8912896 | tf_op jit(solution)/shard_map/dot_general | solution.py:241
  85.3 1.4 %collective-permute-start.28 = (bf16[512,512]{1,0:T(8,128)(2,1)S(1)}, bf16[512,512]{1,0:T(8,128)(2,1)S(1)}, u32[]{:S(2)}, u32[]{:S(2)}) collective-permute-start(bf16[512,512]{1,0:T(8,128)(2,1)S(1)} %convolution_convert_fusion), channel_id=1, source_target_pairs={{0,1},{1,0},{2,3},{3,2},{4,5},{5,4},{6,7},{7,6},{8,9},{9,8},{10,11... | collective-permute-start | bytes 1572872 | tf_op jit(solution)/shard_map/ppermute | solution.py:265
  87.2 0.9 collective-permute-done.23.refs_3_
  88.2 5.6 %cross_spectra.6 = bf16[16,32,4096]{2,1,0:T(8,128)(2,1)S(1)} custom-call(s32[1]{0:T(128)} %bitcast.place, bf16[2,8,2,16,256]{4,3,2,1,0:T(8,128)(2,1)S(1)} %pad_maximum_fusion.5.refs_0_, bf16[2,8,2,16,256]{4,3,2,1,0:T(8,128)(2,1)S(1)} %collective-permute-done.21.refs_1_, bf16[2,8,2,16,256]{4,3,2,1,0:T(8,128)(2,1)S(1)} %collective-permute-done.22.refs_2_, ...), custom_call_target="tpu_custom_call" | custom-call | flops 67108864 | bytes 1048576 | tf_op jit(solution)/shard_map/jit(cross_spectra)/pallas_call | solution.py:98
  93.7 5.6 %cross_spectra.7 = bf16[16,32,4096]{2,1,0:T(8,128)(2,1)S(1)} custom-call(s32[1]{0:T(128)} %bitcast.17.place, bf16[2,8,2,16,256]{4,3,2,1,0:T(8,128)(2,1)S(1)} %pad_maximum_fusion.7.refs_0_, bf16[2,8,2,16,256]{4,3,2,1,0:T(8,128)(2,1)S(1)} %collective-permute-done.25.refs_1_, bf16[2,8,2,16,256]{4,3,2,1,0:T(8,128)(2,1)S(1)} %collective-permute-done.26.refs_2_, ...), custom_call_target="tpu_custom_call" | custom-call | flops 67108864 | bytes 1048576 | tf_op jit(solution)/shard_map/jit(cross_spectra)/pallas_call | solution.py:98
  99.3 2.3 %fusion.14 = f32[512,512]{1,0:T(8,128)S(1)} fusion(bf16[512,4096]{1,0:T(8,128)(2,1)S(1)} %bitcast.63, bf16[4096,512]{1,0:T(8,128)(2,1)S(1)} %copy-done.12), kind=kOutput, calls=%fused_computation.58 | convolution fusion | flops 2147483648 | bytes 9437184 | tf_op jit(solution)/shard_map/dot_general | solution.py:241
  101.7 2.3 %fusion.13 = f32[512,512]{1,0:T(8,128)S(1)} fusion(bf16[512,4096]{1,0:T(8,128)(2,1)S(1)} %bitcast.62, bf16[4096,512]{1,0:T(8,128)(2,1)S(1)} %copy-done.12), kind=kOutput, calls=%fused_computation.57 | convolution fusion | flops 2147483648 | bytes 9437184 | tf_op jit(solution)/shard_map/dot_general | solution.py:241
  104.3 1.5 %pad_maximum_fusion = f32[16,2,32,512]{3,2,1,0:T(8,128)} fusion(f32[16,1,32,512]{3,2,1,0:T(8,128)S(1)} %bitcast.70, f32[16,1,32,512]{3,2,1,0:T(8,128)S(1)} %bitcast.69), kind=kLoop, calls=%fused_computation.4 | loop fusion | flops 524288 | bytes 4194304 | tf_op jit(solution)/shard_map/stack | solution.py:278
  (79 shorter events, 5.1 us)
Async XLA Ops:
  0.0 4.2 %copy-start.11 = (s32[32]{0:T(128)S(1)}, s32[32]{0:T(128)}, u32[]{:S(2)}) copy-start(s32[32]{0:T(128)} %param.6) | copy-start | bytes 388
  0.0 4.8 %copy-start.10 = (s32[2]{0:T(128)S(1)}, s32[2]{0:T(128)}, u32[]{:S(2)}) copy-start(s32[2]{0:T(128)} %param.5) | copy-start | bytes 28
  2.5 8.4 %copy-start = (bf16[8,32,2,2048]{3,1,2,0:T(8,128)(2,1)}, bf16[8,32,2,2048]{3,1,2,0:T(8,128)(2,1)S(1)}, u32[]{:S(2)}) copy-start(bf16[8,32,2,2048]{3,1,2,0:T(8,128)(2,1)S(1)} %copy.9) | copy-start | bytes 6291460
  3.7 3.1 %collective-permute-start.1 = (bf16[8,2,32,1024]{3,2,1,0:T(8,128)(2,1)}, bf16[8,2,32,1024]{3,2,1,0:T(8,128)(2,1)S(1)}, u32[]{:S(2)}, u32[]{:S(2)}) collective-permute-start(bf16[8,2,32,1024]{3,2,1,0:T(8,128)(2,1)} %constant_dynamic-slice_fusion.8), channel_id=1, source_target_pairs={{0,2},{2,0},{4,6},{6,4},{8,10},{10,8},{12,14},{14,12},{16,18},{18,... | collective-permute-start | bytes 3145736 | tf_op jit(solution)/shard_map/ppermute | solution.py:127
  4.7 2.1 %collective-permute-start = (f32[8,32]{1,0:T(8,128)S(1)}, f32[8,32]{1,0:T(8,128)S(1)}, u32[]{:S(2)}, u32[]{:S(2)}) collective-permute-start(f32[8,32]{1,0:T(8,128)S(1)} %rsqrt_multiply_fusion), channel_id=1, source_target_pairs={{0,2},{2,0},{4,6},{6,4},{8,10},{10,8},{12,14},{14,12},{16,18},{18,... | collective-permute-start | bytes 3080 | tf_op jit(solution)/shard_map/ppermute | solution.py:127
  10.9 33.9 %copy-start.3 = (bf16[8,2,32,512]{3,2,1,0:T(8,128)(2,1)S(1)}, bf16[8,2,32,512]{3,2,1,0:T(8,128)(2,1)}, u32[]{:S(2)}) copy-start(bf16[8,2,32,512]{3,2,1,0:T(8,128)(2,1)} %get-tuple-element.112) | copy-start | bytes 1572868
  10.9 36.3 %copy-start.2 = (bf16[8,2,32,512]{3,2,1,0:T(8,128)(2,1)S(1)}, bf16[8,2,32,512]{3,2,1,0:T(8,128)(2,1)}, u32[]{:S(2)}) copy-start(bf16[8,2,32,512]{3,2,1,0:T(8,128)(2,1)} %get-tuple-element.107) | copy-start | bytes 1572868
  11.4 9.5 %collective-permute-start.2 = (bf16[8,2,16,512]{3,2,1,0:T(8,128)(2,1)S(1)}, bf16[8,2,16,512]{3,2,1,0:T(8,128)(2,1)S(1)}, u32[]{:S(2)}, u32[]{:S(2)}) collective-permute-start(bf16[8,2,16,512]{3,2,1,0:T(8,128)(2,1)S(1)} %get-tuple-element.62), channel_id=1, source_target_pairs={{0,4},{2,6},{4,0},{6,2},{8,12},{10,14},{12,8},{14,10},{16,20},{18,... | collective-permute-start | bytes 786440 | tf_op jit(solution)/shard_map/ppermute | solution.py:127
  14.4 7.9 %collective-permute-start.3 = (bf16[8,2,16,512]{3,2,1,0:T(8,128)(2,1)S(1)}, bf16[8,2,16,512]{3,2,1,0:T(8,128)(2,1)S(1)}, u32[]{:S(2)}, u32[]{:S(2)}) collective-permute-start(bf16[8,2,16,512]{3,2,1,0:T(8,128)(2,1)S(1)} %get-tuple-element.63), channel_id=1, source_target_pairs={{0,8},{2,10},{4,12},{6,14},{8,0},{10,2},{12,4},{14,6},{16,24},{18,... | collective-permute-start | bytes 786440 | tf_op jit(solution)/shard_map/ppermute | solution.py:127
  23.6 5.0 %collective-permute-start.4 = (bf16[8,2,16,256]{3,2,1,0:T(8,128)(2,1)S(1)}, bf16[8,2,16,256]{3,2,1,0:T(8,128)(2,1)S(1)}, u32[]{:S(2)}, u32[]{:S(2)}) collective-permute-start(bf16[8,2,16,256]{3,2,1,0:T(8,128)(2,1)S(1)} %constant_dynamic-slice_fusion.3), channel_id=1, source_target_pairs={{0,8},{2,10},{4,12},{6,14},{8,0},{10,2},{12,4},{14,6},{16,24},{18,... | collective-permute-start | bytes 393224 | tf_op jit(solution)/shard_map/ppermute | solution.py:127
  26.3 31.7 %copy-start.1 = (bf16[8,32,2,2048]{3,1,2,0:T(8,128)(2,1)S(1)}, bf16[8,32,2,2048]{3,1,2,0:T(8,128)(2,1)}, u32[]{:S(2)}) copy-start(bf16[8,32,2,2048]{3,1,2,0:T(8,128)(2,1)} %copy-done) | copy-start | bytes 6291460
  26.4 5.0 %collective-permute-start.5 = (bf16[8,2,16,256]{3,2,1,0:T(8,128)(2,1)S(1)}, bf16[8,2,16,256]{3,2,1,0:T(8,128)(2,1)S(1)}, u32[]{:S(2)}, u32[]{:S(2)}) collective-permute-start(bf16[8,2,16,256]{3,2,1,0:T(8,128)(2,1)S(1)} %constant_dynamic-slice_fusion.2), channel_id=1, source_target_pairs={{0,4},{2,6},{4,0},{6,2},{8,12},{10,14},{12,8},{14,10},{16,20},{18,... | collective-permute-start | bytes 393224 | tf_op jit(solution)/shard_map/ppermute | solution.py:127
  31.6 12.3 %collective-permute-start.10 = (bf16[2,8,2,16,256]{4,3,2,1,0:T(8,128)(2,1)S(1)}, bf16[2,8,2,16,256]{4,3,2,1,0:T(8,128)(2,1)S(1)}, u32[]{:S(2)}, u32[]{:S(2)}) collective-permute-start(bf16[2,8,2,16,256]{4,3,2,1,0:T(8,128)(2,1)S(1)} %pad_maximum_fusion.3), channel_id=1, source_target_pairs={{0,16},{2,18},{4,20},{6,22},{8,24},{10,26},{12,28},{14,30},{16,0},... | collective-permute-start | bytes 786440 | tf_op jit(solution)/shard_map/ppermute | solution.py:127
  34.2 10.6 %collective-permute-start.6 = (bf16[8,2,16,512]{3,2,1,0:T(8,128)(2,1)S(1)}, bf16[8,2,16,512]{3,2,1,0:T(8,128)(2,1)S(1)}, u32[]{:S(2)}, u32[]{:S(2)}) collective-permute-start(bf16[8,2,16,512]{3,2,1,0:T(8,128)(2,1)S(1)} %get-tuple-element.77), channel_id=1, source_target_pairs={{0,4},{2,6},{4,0},{6,2},{8,12},{10,14},{12,8},{14,10},{16,20},{18,... | collective-permute-start | bytes 786440 | tf_op jit(solution)/shard_map/ppermute | solution.py:127
  34.8 12.4 %collective-permute-start.8 = (bf16[8,2,16,512]{3,2,1,0:T(8,128)(2,1)S(1)}, bf16[8,2,16,512]{3,2,1,0:T(8,128)(2,1)S(1)}, u32[]{:S(2)}, u32[]{:S(2)}) collective-permute-start(bf16[8,2,16,512]{3,2,1,0:T(8,128)(2,1)S(1)} %get-tuple-element.81), channel_id=1, source_target_pairs={{0,8},{2,10},{4,12},{6,14},{8,0},{10,2},{12,4},{14,6},{16,24},{18,... | collective-permute-start | bytes 786440 | tf_op jit(solution)/shard_map/ppermute | solution.py:127
  44.2 5.6 %collective-permute-start.13 = (bf16[1,8,2,16,256]{4,3,2,1,0:T(8,128)(2,1)S(1)}, bf16[1,8,2,16,256]{4,3,2,1,0:T(8,128)(2,1)S(1)}, u32[]{:S(2)}, u32[]{:S(2)}) collective-permute-start(bf16[1,8,2,16,256]{4,3,2,1,0:T(8,128)(2,1)S(1)} %get-tuple-element.119), channel_id=1, source_target_pairs={{0,4},{2,6},{4,0},{6,2},{8,12},{10,14},{12,8},{14,10},{16,20},{18,... | collective-permute-start | bytes 393224 | tf_op jit(solution)/shard_map/ppermute | solution.py:127
  44.8 6.0 %collective-permute-start.12 = (bf16[1,8,2,16,256]{4,3,2,1,0:T(8,128)(2,1)S(1)}, bf16[1,8,2,16,256]{4,3,2,1,0:T(8,128)(2,1)S(1)}, u32[]{:S(2)}, u32[]{:S(2)}) collective-permute-start(bf16[1,8,2,16,256]{4,3,2,1,0:T(8,128)(2,1)S(1)} %get-tuple-element.120), channel_id=1, source_target_pairs={{0,8},{2,10},{4,12},{6,14},{8,0},{10,2},{12,4},{14,6},{16,24},{18,... | collective-permute-start | bytes 393224 | tf_op jit(solution)/shard_map/ppermute | solution.py:127
  44.9 12.9 %copy-start.4 = (bf16[8,2,16,512]{3,2,1,0:T(8,128)(2,1)}, bf16[8,2,16,512]{3,2,1,0:T(8,128)(2,1)S(1)}, u32[]{:S(2)}) copy-start(bf16[8,2,16,512]{3,2,1,0:T(8,128)(2,1)S(1)} %dynamic-slice_select_fusion.3) | copy-start | bytes 786436
  45.1 7.7 %collective-permute-start.7 = (bf16[8,2,16,256]{3,2,1,0:T(8,128)(2,1)S(1)}, bf16[8,2,16,256]{3,2,1,0:T(8,128)(2,1)S(1)}, u32[]{:S(2)}, u32[]{:S(2)}) collective-permute-start(bf16[8,2,16,256]{3,2,1,0:T(8,128)(2,1)S(1)} %constant_dynamic-slice_fusion), channel_id=1, source_target_pairs={{0,8},{2,10},{4,12},{6,14},{8,0},{10,2},{12,4},{14,6},{16,24},{18,... | collective-permute-start | bytes 393224 | tf_op jit(solution)/shard_map/ppermute | solution.py:127
  47.3 10.6 %copy-start.6 = (bf16[8,2,16,512]{3,2,1,0:T(8,128)(2,1)}, bf16[8,2,16,512]{3,2,1,0:T(8,128)(2,1)S(1)}, u32[]{:S(2)}) copy-start(bf16[8,2,16,512]{3,2,1,0:T(8,128)(2,1)S(1)} %dynamic-slice_select_fusion) | copy-start | bytes 786436
  47.4 6.4 %collective-permute-start.9 = (bf16[8,2,16,256]{3,2,1,0:T(8,128)(2,1)S(1)}, bf16[8,2,16,256]{3,2,1,0:T(8,128)(2,1)S(1)}, u32[]{:S(2)}, u32[]{:S(2)}) collective-permute-start(bf16[8,2,16,256]{3,2,1,0:T(8,128)(2,1)S(1)} %constant_dynamic-slice_fusion.6), channel_id=1, source_target_pairs={{0,4},{2,6},{4,0},{6,2},{8,12},{10,14},{12,8},{14,10},{16,20},{18,... | collective-permute-start | bytes 393224 | tf_op jit(solution)/shard_map/ppermute | solution.py:127
  50.8 7.0 %collective-permute-start.14 = (bf16[2,8,2,16,256]{4,3,2,1,0:T(8,128)(2,1)S(1)}, bf16[2,8,2,16,256]{4,3,2,1,0:T(8,128)(2,1)S(1)}, u32[]{:S(2)}, u32[]{:S(2)}) collective-permute-start(bf16[2,8,2,16,256]{4,3,2,1,0:T(8,128)(2,1)S(1)} %pad_maximum_fusion.4), channel_id=1, source_target_pairs={{0,4},{2,6},{4,0},{6,2},{8,12},{10,14},{12,8},{14,10},{16,20},{18,... | collective-permute-start | bytes 786440 | tf_op jit(solution)/shard_map/ppermute | solution.py:127
  52.2 13.2 %collective-permute-start.18 = (bf16[2,8,2,16,256]{4,3,2,1,0:T(8,128)(2,1)S(1)}, bf16[2,8,2,16,256]{4,3,2,1,0:T(8,128)(2,1)}, u32[]{:S(2)}, u32[]{:S(2)}) collective-permute-start(bf16[2,8,2,16,256]{4,3,2,1,0:T(8,128)(2,1)S(1)} %pad_maximum_fusion.6.refs_0_), channel_id=1, source_target_pairs={{0,8},{2,10},{4,12},{6,14},{8,0},{10,2},{12,4},{14,6},{16,24},{18,... | collective-permute-start | bytes 786440 | tf_op jit(solution)/shard_map/ppermute | solution.py:127
  53.9 4.0 %copy-start.8 = (bf16[8,2,16,256]{3,2,1,0:T(8,128)(2,1)}, bf16[8,2,16,256]{3,2,1,0:T(8,128)(2,1)S(1)}, u32[]{:S(2)}) copy-start(bf16[8,2,16,256]{3,2,1,0:T(8,128)(2,1)S(1)} %collective-permute-done.9) | copy-start | bytes 393220
  54.7 11.9 %collective-permute-start.11 = (bf16[2,8,2,16,256]{4,3,2,1,0:T(8,128)(2,1)}, bf16[2,8,2,16,256]{4,3,2,1,0:T(8,128)(2,1)}, u32[]{:S(2)}, u32[]{:S(2)}) collective-permute-start(bf16[2,8,2,16,256]{4,3,2,1,0:T(8,128)(2,1)} %pad_maximum_fusion.2), channel_id=1, source_target_pairs={{0,16},{2,18},{4,20},{6,22},{8,24},{10,26},{12,28},{14,30},{16,0},... | collective-permute-start | bytes 786440 | tf_op jit(solution)/shard_map/ppermute | solution.py:127
  57.9 2.0 %collective-permute-start.15 = (bf16[4,8,2,16,256]{4,3,2,1,0:T(8,128)(2,1)S(1)}, bf16[4,8,2,16,256]{4,3,2,1,0:T(8,128)(2,1)S(1)}, u32[]{:S(2)}, u32[]{:S(2)}) collective-permute-start(bf16[4,8,2,16,256]{4,3,2,1,0:T(8,128)(2,1)S(1)} %pad_maximum_fusion.1.refs_0_), channel_id=1, source_target_pairs={{0,2},{2,0},{4,6},{6,4},{8,10},{10,8},{12,14},{14,12},{16,18},{18,... | collective-permute-start | bytes 1572872 | tf_op jit(solution)/shard_map/ppermute | solution.py:127
  58.6 8.0 %copy-start.5 = (bf16[8,2,16,512]{3,2,1,0:T(8,128)(2,1)S(1)}, bf16[8,2,16,512]{3,2,1,0:T(8,128)(2,1)}, u32[]{:S(2)}) copy-start(bf16[8,2,16,512]{3,2,1,0:T(8,128)(2,1)} %copy-done.4) | copy-start | bytes 786436
  58.6 8.0 %copy-start.7 = (bf16[8,2,16,512]{3,2,1,0:T(8,128)(2,1)S(1)}, bf16[8,2,16,512]{3,2,1,0:T(8,128)(2,1)}, u32[]{:S(2)}) copy-start(bf16[8,2,16,512]{3,2,1,0:T(8,128)(2,1)} %copy-done.6) | copy-start | bytes 786436
  58.7 8.0 %copy-start.9 = (bf16[8,2,16,256]{3,2,1,0:T(8,128)(2,1)S(1)}, bf16[8,2,16,256]{3,2,1,0:T(8,128)(2,1)}, u32[]{:S(2)}) copy-start(bf16[8,2,16,256]{3,2,1,0:T(8,128)(2,1)} %copy-done.8) | copy-start | bytes 393220
  58.7 16.7 %collective-permute-start.19 = (bf16[2,8,2,16,256]{4,3,2,1,0:T(8,128)(2,1)S(1)}, bf16[2,8,2,16,256]{4,3,2,1,0:T(8,128)(2,1)S(1)}, u32[]{:S(2)}, u32[]{:S(2)}) collective-permute-start(bf16[2,8,2,16,256]{4,3,2,1,0:T(8,128)(2,1)S(1)} %pad_maximum_fusion.6.refs_0_), channel_id=1, source_target_pairs={{0,2},{2,0},{4,6},{6,4},{8,10},{10,8},{12,14},{14,12},{16,18},{18,... | collective-permute-start | bytes 786440 | tf_op jit(solution)/shard_map/ppermute | solution.py:127
  59.9 9.1 %copy-start.12 = (bf16[4096,512]{1,0:T(8,128)(2,1)S(1)}, bf16[4096,512]{1,0:T(8,128)(2,1)}, u32[]{:S(2)}) copy-start(bf16[4096,512]{1,0:T(8,128)(2,1)} %constant.107.clone) | copy-start | bytes 12582916
  67.8 5.1 %collective-permute-start.16 = (bf16[1,8,2,16,256]{4,3,2,1,0:T(8,128)(2,1)S(1)}, bf16[1,8,2,16,256]{4,3,2,1,0:T(8,128)(2,1)S(1)}, u32[]{:S(2)}, u32[]{:S(2)}) collective-permute-start(bf16[1,8,2,16,256]{4,3,2,1,0:T(8,128)(2,1)S(1)} %get-tuple-element.88), channel_id=1, source_target_pairs={{0,8},{2,10},{4,12},{6,14},{8,0},{10,2},{12,4},{14,6},{16,24},{18,... | collective-permute-start | bytes 393224 | tf_op jit(solution)/shard_map/ppermute | solution.py:127
  67.9 5.0 %collective-permute-start.17 = (bf16[1,8,2,16,256]{4,3,2,1,0:T(8,128)(2,1)S(1)}, bf16[1,8,2,16,256]{4,3,2,1,0:T(8,128)(2,1)S(1)}, u32[]{:S(2)}, u32[]{:S(2)}) collective-permute-start(bf16[1,8,2,16,256]{4,3,2,1,0:T(8,128)(2,1)S(1)} %get-tuple-element.89), channel_id=1, source_target_pairs={{0,4},{2,6},{4,0},{6,2},{8,12},{10,14},{12,8},{14,10},{16,20},{18,... | collective-permute-start | bytes 393224 | tf_op jit(solution)/shard_map/ppermute | solution.py:127
  69.0 7.5 %collective-permute-start.20 = (bf16[2,8,2,16,256]{4,3,2,1,0:T(8,128)(2,1)}, bf16[2,8,2,16,256]{4,3,2,1,0:T(8,128)(2,1)S(1)}, u32[]{:S(2)}, u32[]{:S(2)}) collective-permute-start(bf16[2,8,2,16,256]{4,3,2,1,0:T(8,128)(2,1)} %collective-permute-done.18.refs_1_), channel_id=1, source_target_pairs={{0,2},{2,0},{4,6},{6,4},{8,10},{10,8},{12,14},{14,12},{16,18},{18,... | collective-permute-start | bytes 786440 | tf_op jit(solution)/shard_map/ppermute | solution.py:127
  71.3 22.4 %collective-permute-start.24 = (bf16[512,512]{1,0:T(8,128)(2,1)S(1)}, bf16[512,512]{1,0:T(8,128)(2,1)S(1)}, u32[]{:S(2)}, u32[]{:S(2)}) collective-permute-start(bf16[512,512]{1,0:T(8,128)(2,1)S(1)} %convolution_convert_fusion.1), channel_id=1, source_target_pairs={{0,1},{1,0},{2,3},{3,2},{4,5},{5,4},{6,7},{7,6},{8,9},{9,8},{10,11... | collective-permute-start | bytes 1572872 | tf_op jit(solution)/shard_map/ppermute | solution.py:265
  73.0 14.1 %collective-permute-start.22 = (bf16[2,8,2,16,256]{4,3,2,1,0:T(8,128)(2,1)S(1)}, bf16[2,8,2,16,256]{4,3,2,1,0:T(8,128)(2,1)S(1)}, u32[]{:S(2)}, u32[]{:S(2)}) collective-permute-start(bf16[2,8,2,16,256]{4,3,2,1,0:T(8,128)(2,1)S(1)} %pad_maximum_fusion.5.refs_0_), channel_id=1, source_target_pairs={{0,2},{2,0},{4,6},{6,4},{8,10},{10,8},{12,14},{14,12},{16,18},{18,... | collective-permute-start | bytes 786440 | tf_op jit(solution)/shard_map/ppermute | solution.py:127
  73.3 13.3 %collective-permute-start.25 = (bf16[2,8,2,16,256]{4,3,2,1,0:T(8,128)(2,1)S(1)}, bf16[2,8,2,16,256]{4,3,2,1,0:T(8,128)(2,1)S(1)}, u32[]{:S(2)}, u32[]{:S(2)}) collective-permute-start(bf16[2,8,2,16,256]{4,3,2,1,0:T(8,128)(2,1)S(1)} %pad_maximum_fusion.7.refs_0_), channel_id=1, source_target_pairs={{0,8},{2,10},{4,12},{6,14},{8,0},{10,2},{12,4},{14,6},{16,24},{18,... | collective-permute-start | bytes 786440 | tf_op jit(solution)/shard_map/ppermute | solution.py:127
  75.3 11.3 %collective-permute-start.21 = (bf16[2,8,2,16,256]{4,3,2,1,0:T(8,128)(2,1)S(1)}, bf16[2,8,2,16,256]{4,3,2,1,0:T(8,128)(2,1)S(1)}, u32[]{:S(2)}, u32[]{:S(2)}) collective-permute-start(bf16[2,8,2,16,256]{4,3,2,1,0:T(8,128)(2,1)S(1)} %pad_maximum_fusion.5.refs_0_), channel_id=1, source_target_pairs={{0,4},{2,6},{4,0},{6,2},{8,12},{10,14},{12,8},{14,10},{16,20},{18,... | collective-permute-start | bytes 786440 | tf_op jit(solution)/shard_map/ppermute | solution.py:127
  85.3 14.1 %collective-permute-start.28 = (bf16[512,512]{1,0:T(8,128)(2,1)S(1)}, bf16[512,512]{1,0:T(8,128)(2,1)S(1)}, u32[]{:S(2)}, u32[]{:S(2)}) collective-permute-start(bf16[512,512]{1,0:T(8,128)(2,1)S(1)} %convolution_convert_fusion), channel_id=1, source_target_pairs={{0,1},{1,0},{2,3},{3,2},{4,5},{5,4},{6,7},{7,6},{8,9},{9,8},{10,11... | collective-permute-start | bytes 1572872 | tf_op jit(solution)/shard_map/ppermute | solution.py:265
  86.6 1.5 %collective-permute-start.23 = (bf16[2,8,2,16,256]{4,3,2,1,0:T(8,128)(2,1)S(1)}, bf16[2,8,2,16,256]{4,3,2,1,0:T(8,128)(2,1)S(1)}, u32[]{:S(2)}, u32[]{:S(2)}) collective-permute-start(bf16[2,8,2,16,256]{4,3,2,1,0:T(8,128)(2,1)S(1)} %collective-permute-done.21.refs_1_), channel_id=1, source_target_pairs={{0,2},{2,0},{4,6},{6,4},{8,10},{10,8},{12,14},{14,12},{16,18},{18,... | collective-permute-start | bytes 786440 | tf_op jit(solution)/shard_map/ppermute | solution.py:127
  86.6 7.1 %collective-permute-start.26 = (bf16[2,8,2,16,256]{4,3,2,1,0:T(8,128)(2,1)S(1)}, bf16[2,8,2,16,256]{4,3,2,1,0:T(8,128)(2,1)S(1)}, u32[]{:S(2)}, u32[]{:S(2)}) collective-permute-start(bf16[2,8,2,16,256]{4,3,2,1,0:T(8,128)(2,1)S(1)} %pad_maximum_fusion.7.refs_0_), channel_id=1, source_target_pairs={{0,2},{2,0},{4,6},{6,4},{8,10},{10,8},{12,14},{14,12},{16,18},{18,... | collective-permute-start | bytes 786440 | tf_op jit(solution)/shard_map/ppermute | solution.py:127
  87.1 6.6 %collective-permute-start.27 = (bf16[2,8,2,16,256]{4,3,2,1,0:T(8,128)(2,1)S(1)}, bf16[2,8,2,16,256]{4,3,2,1,0:T(8,128)(2,1)S(1)}, u32[]{:S(2)}, u32[]{:S(2)}) collective-permute-start(bf16[2,8,2,16,256]{4,3,2,1,0:T(8,128)(2,1)S(1)} %collective-permute-done.25.refs_1_), channel_id=1, source_target_pairs={{0,2},{2,0},{4,6},{6,4},{8,10},{10,8},{12,14},{14,12},{16,18},{18,... | collective-permute-start | bytes 786440 | tf_op jit(solution)/shard_map/ppermute | solution.py:127
where the time goes:
time: 106 us
  starting transfers between devices  27.6 us (26%)
  waiting for transfers between devices  26.4 us (25%)
  Pallas kernels  23.2 us (22%)
  other arithmetic  12.3 us (12%)
  matrix products  9.3 us (9%)
  local copies, waits for them, and re-layouts  5.38 us (5%)
  between operations  1.7 us (2%)
    ppermute x27, waiting for transfers between devices, per_device(): lax.ppermute(value, 'chan', [(i, i ^ 1 << place) for i in range(chan)])  26.4 us
    ppermute x27, starting transfers between devices, per_device(): lax.ppermute(value, 'chan', [(i, i ^ 1 << place) for i in range(chan)])  24.6 us
    pallas_call x4, Pallas kernels, cross_spectra(): pl.pallas_call(cross_kernel, in_specs=[pl.BlockSpec(memory_space=pltpu.SM...  23.2 us
    dot_general x4, matrix products, lags(): jnp.dot(cross.reshape(kept * channels, 2 * num_bins), table, preferred_el...  9.3 us
    convert_element_type x1, other arithmetic, chosen(): value = cut(value.astype(jnp.bfloat16), 2, first_rows[part], kept)  4.09 us
    ppermute x2, starting transfers between devices, per_device(): come = [lax.ppermute(value, 'tm', partners) for value in sent]  3.04 us
    unnamed x27, local copies, waits for them, and re-layouts  2.56 us
    select_n x4, other arithmetic, broadcast(): jnp.where(same[first][step], chosen(step, part, first, 0), have[step])  2.38 us
  transfers between devices with their start and end apart: 29, of which 12 were waited for; matrix products, arithmetic and copies ran while one was open for 10% of the time, Pallas kernels for 22%

commit v1 on v0

--- a/solution.py
+++ b/solution.py
@@ -137,9 +137,9 @@
 
     raw = lax.optimization_barrier(spectra.transpose(0, 2, 1, 3))
     half = num_bins // 2
-    own_half = (me & 1) * half
-    mine = cut(raw, 3, own_half, half)
-    given = swap(cut(raw, 3, half - own_half, half), 0)
+    own_half = me & 1
+    mine = cut(raw, 3, own_half * half, half)
+    given = swap(cut(raw, 3, (own_half ^ 1) * half, half), 0)
     usable = quality.astype(jnp.float32)[None, :]
     wide = raw.astype(jnp.float32)
     power = jnp.mean(wide * wide, axis=(1, 3)) * usable
@@ -154,8 +154,8 @@
     def starts_of(size):
         out = []
         for place in (1, 2):
-            own = (me & (1 << place)) * (size >> place)
-            out.append([own, size - own])
+            own = me & (1 << place)
+            out.append([own * (size >> place), (own ^ (1 << place)) * (size >> place)])
         return out
 
     def same_side(place):

time: 106 us -> 106 us (level)
  no operation moved by 1% of the time
where the time goes in v1:
time: 106 us
  starting transfers between devices  27.6 us (26%)
  waiting for transfers between devices  26.4 us (25%)
  Pallas kernels  23.2 us (22%)
  other arithmetic  12.3 us (12%)
  matrix products  9.29 us (9%)
  local copies, waits for them, and re-layouts  5.38 us (5%)
  between operations  1.69 us (2%)
    ppermute x27, waiting for transfers between devices, per_device(): lax.ppermute(value, 'chan', [(i, i ^ 1 << place) for i in range(chan)])  26.4 us
    ppermute x27, starting transfers between devices, per_device(): lax.ppermute(value, 'chan', [(i, i ^ 1 << place) for i in range(chan)])  24.6 us
    pallas_call x4, Pallas kernels, cross_spectra(): pl.pallas_call(cross_kernel, in_specs=[pl.BlockSpec(memory_space=pltpu.SM...  23.2 us
    dot_general x4, matrix products, lags(): jnp.dot(cross.reshape(kept * channels, 2 * num_bins), table, preferred_el...  9.29 us
    convert_element_type x1, other arithmetic, chosen(): value = cut(value.astype(jnp.bfloat16), 2, first_rows[part], kept)  4.09 us
    ppermute x2, starting transfers between devices, per_device(): come = [lax.ppermute(value, 'tm', partners) for value in sent]  3.03 us
    unnamed x27, local copies, waits for them, and re-layouts  2.56 us
    select_n x4, other arithmetic, broadcast(): jnp.where(same[first][step], chosen(step, part, first, 0), have[step])  2.38 us
  transfers between devices with their start and end apart: 29, of which 12 were waited for; matrix products, arithmetic and copies ran while one was open for 10% of the time, Pallas kernels for 22%

profile of v1, /device:TPU:0, one launch (start us, length us, event | category | flops | bytes accessed | tf_op | source)
XLA Modules:
  0.0 105.8 jit_solution(1455860159535203373)
XLA Ops:
  0.0 2.5 %copy.9 = bf16[8,32,2,2048]{3,1,2,0:T(8,128)(2,1)S(1)} copy(bf16[8,32,2,2048]{3,2,1,0:T(2,128)(2,1)} %param.4) | data formatting | bytes 4194304 | tf_op args[0]
  2.5 1.2 %constant_dynamic-slice_fusion.8 = bf16[8,2,32,1024]{3,2,1,0:T(8,128)(2,1)} fusion(bf16[8,2,32,2048]{3,2,1,0:T(8,128)(2,1)S(1)} %bitcast.65, s32[]{:T(128)S(6)} %mul.134), kind=kLoop, calls=%fused_computation.51 | loop fusion | bytes 2097156 | tf_op jit(solution)/shard_map/dynamic_slice | solution.py:136
  4.8 0.7 fusion.12
  6.8 4.1 %multiply_convert_fusion = (bf16[8,2,32,512]{3,2,1,0:T(8,128)(2,1)}, bf16[8,2,32,512]{3,2,1,0:T(8,128)(2,1)S(1)}, bf16[8,2,32,512]{3,2,1,0:T(8,128)(2,1)S(1)}, bf16[8,2,32,512]{3,2,1,0:T(8,128)(2,1)}) fusion(bf16[8,2,32,1024]{3,2,1,0:T(8,128)(2,1)S(1)} %collective-permute-done.1, s32[]{:T(128)S(6)} %mul.128, bf16[8,2,32,2048]{3,2,1,0:T(8,128)(2,1)S(1)} %bitcast.67, ...), kind=kLoop, calls=%fused_computation.10 | loop fusion | flops 4194304 | bytes 6293538 | tf_op jit(solution)/shard_map/convert_element_type | solution.py:185
  11.4 3.0 %collective-permute-start.2 = (bf16[8,2,16,512]{3,2,1,0:T(8,128)(2,1)S(1)}, bf16[8,2,16,512]{3,2,1,0:T(8,128)(2,1)S(1)}, u32[]{:S(2)}, u32[]{:S(2)}) collective-permute-start(bf16[8,2,16,512]{3,2,1,0:T(8,128)(2,1)S(1)} %get-tuple-element.62), channel_id=1, source_target_pairs={{0,4},{2,6},{4,0},{6,2},{8,12},{10,14},{12,8},{14,10},{16,20},{18,... | collective-permute-start | bytes 786440 | tf_op jit(solution)/shard_map/ppermute | solution.py:127
  14.4 1.6 %collective-permute-start.3 = (bf16[8,2,16,512]{3,2,1,0:T(8,128)(2,1)S(1)}, bf16[8,2,16,512]{3,2,1,0:T(8,128)(2,1)S(1)}, u32[]{:S(2)}, u32[]{:S(2)}) collective-permute-start(bf16[8,2,16,512]{3,2,1,0:T(8,128)(2,1)S(1)} %get-tuple-element.63), channel_id=1, source_target_pairs={{0,8},{2,10},{4,12},{6,14},{8,0},{10,2},{12,4},{14,6},{16,24},{18,... | collective-permute-start | bytes 786440 | tf_op jit(solution)/shard_map/ppermute | solution.py:127
  16.0 4.9 %collective-permute-done.2 = bf16[8,2,16,512]{3,2,1,0:T(8,128)(2,1)S(1)} collective-permute-done((bf16[8,2,16,512]{3,2,1,0:T(8,128)(2,1)S(1)}, bf16[8,2,16,512]{3,2,1,0:T(8,128)(2,1)S(1)}, u32[]{:S(2)}, u32[]{:S(2)}) %collective-permute-start.2) | collective-permute-done | bytes 262176 | tf_op jit(solution)/shard_map/ppermute | solution.py:127
  20.9 1.5 %collective-permute-done.3 = bf16[8,2,16,512]{3,2,1,0:T(8,128)(2,1)S(1)} collective-permute-done((bf16[8,2,16,512]{3,2,1,0:T(8,128)(2,1)S(1)}, bf16[8,2,16,512]{3,2,1,0:T(8,128)(2,1)S(1)}, u32[]{:S(2)}, u32[]{:S(2)}) %collective-permute-start.3) | collective-permute-done | bytes 262176 | tf_op jit(solution)/shard_map/ppermute | solution.py:127
  22.4 1.1 %dynamic-slice_select_fusion.2 = bf16[8,2,16,512]{3,2,1,0:T(8,128)(2,1)S(1)} fusion(bf16[8,2,16,512]{3,2,1,0:T(8,128)(2,1)S(1)} %collective-permute-done.2, bf16[8,2,32,512]{3,2,1,0:T(8,128)(2,1)} %get-tuple-element.112, s32[]{:T(128)S(6)} %mul.130, pred[]{:T(512)S(6)} %eq.26), kind=kLoop, calls=%fused_computation.23 | loop fusion | flops 131072 | bytes 786437 | tf_op jit(solution)/shard_map/jit(_where)/select_n | solution.py:210
  23.6 1.6 %collective-permute-start.4 = (bf16[8,2,16,256]{3,2,1,0:T(8,128)(2,1)S(1)}, bf16[8,2,16,256]{3,2,1,0:T(8,128)(2,1)S(1)}, u32[]{:S(2)}, u32[]{:S(2)}) collective-permute-start(bf16[8,2,16,256]{3,2,1,0:T(8,128)(2,1)S(1)} %constant_dynamic-slice_fusion.3), channel_id=1, source_target_pairs={{0,8},{2,10},{4,12},{6,14},{8,0},{10,2},{12,4},{14,6},{16,24},{18,... | collective-permute-start | bytes 393224 | tf_op jit(solution)/shard_map/ppermute | solution.py:127
  25.2 1.1 %dynamic-slice_select_fusion.1 = bf16[8,2,16,512]{3,2,1,0:T(8,128)(2,1)S(1)} fusion(bf16[8,2,16,512]{3,2,1,0:T(8,128)(2,1)S(1)} %collective-permute-done.3, bf16[8,2,32,512]{3,2,1,0:T(8,128)(2,1)} %get-tuple-element.107, s32[]{:T(128)S(6)} %mul.130, pred[]{:T(512)S(6)} %eq.29), kind=kLoop, calls=%fused_computation.22 | loop fusion | flops 131072 | bytes 786437 | tf_op jit(solution)/shard_map/jit(_where)/select_n | solution.py:210
  26.4 0.6 collective-permute-start.5
  27.0 1.6 %collective-permute-done.4 = bf16[8,2,16,256]{3,2,1,0:T(8,128)(2,1)S(1)} collective-permute-done((bf16[8,2,16,256]{3,2,1,0:T(8,128)(2,1)S(1)}, bf16[8,2,16,256]{3,2,1,0:T(8,128)(2,1)S(1)}, u32[]{:S(2)}, u32[]{:S(2)}) %collective-permute-start.4) | collective-permute-done | bytes 131104 | tf_op jit(solution)/shard_map/ppermute | solution.py:127
  28.7 2.7 %collective-permute-done.5 = bf16[8,2,16,256]{3,2,1,0:T(8,128)(2,1)S(1)} collective-permute-done((bf16[8,2,16,256]{3,2,1,0:T(8,128)(2,1)S(1)}, bf16[8,2,16,256]{3,2,1,0:T(8,128)(2,1)S(1)}, u32[]{:S(2)}, u32[]{:S(2)}) %collective-permute-start.5) | collective-permute-done | bytes 131104 | tf_op jit(solution)/shard_map/ppermute | solution.py:127
  31.6 2.7 %collective-permute-start.10 = (bf16[2,8,2,16,256]{4,3,2,1,0:T(8,128)(2,1)S(1)}, bf16[2,8,2,16,256]{4,3,2,1,0:T(8,128)(2,1)S(1)}, u32[]{:S(2)}, u32[]{:S(2)}) collective-permute-start(bf16[2,8,2,16,256]{4,3,2,1,0:T(8,128)(2,1)S(1)} %pad_maximum_fusion.3), channel_id=1, source_target_pairs={{0,16},{2,18},{4,20},{6,22},{8,24},{10,26},{12,28},{14,30},{16,0},... | collective-permute-start | bytes 786440 | tf_op jit(solution)/shard_map/ppermute | solution.py:127
  34.3 0.5 collective-permute-start.6
  35.2 8.7 %collective-permute-done.10 = bf16[2,8,2,16,256]{4,3,2,1,0:T(8,128)(2,1)S(1)} collective-permute-done((bf16[2,8,2,16,256]{4,3,2,1,0:T(8,128)(2,1)S(1)}, bf16[2,8,2,16,256]{4,3,2,1,0:T(8,128)(2,1)S(1)}, u32[]{:S(2)}, u32[]{:S(2)}) %collective-permute-start.10) | collective-permute-done | bytes 262176 | tf_op jit(solution)/shard_map/ppermute | solution.py:127
  44.2 0.6 collective-permute-start.13
  45.1 2.1 %collective-permute-start.7 = (bf16[8,2,16,256]{3,2,1,0:T(8,128)(2,1)S(1)}, bf16[8,2,16,256]{3,2,1,0:T(8,128)(2,1)S(1)}, u32[]{:S(2)}, u32[]{:S(2)}) collective-permute-start(bf16[8,2,16,256]{3,2,1,0:T(8,128)(2,1)S(1)} %constant_dynamic-slice_fusion), channel_id=1, source_target_pairs={{0,8},{2,10},{4,12},{6,14},{8,0},{10,2},{12,4},{14,6},{16,24},{18,... | collective-permute-start | bytes 393224 | tf_op jit(solution)/shard_map/ppermute | solution.py:127
  47.4 1.5 %collective-permute-start.9 = (bf16[8,2,16,256]{3,2,1,0:T(8,128)(2,1)S(1)}, bf16[8,2,16,256]{3,2,1,0:T(8,128)(2,1)S(1)}, u32[]{:S(2)}, u32[]{:S(2)}) collective-permute-start(bf16[8,2,16,256]{3,2,1,0:T(8,128)(2,1)S(1)} %constant_dynamic-slice_fusion.6), channel_id=1, source_target_pairs={{0,4},{2,6},{4,0},{6,2},{8,12},{10,14},{12,8},{14,10},{16,20},{18,... | collective-permute-start | bytes 393224 | tf_op jit(solution)/shard_map/ppermute | solution.py:127
  49.0 0.8 collective-permute-done.13
  49.8 1.0 collective-permute-done.12
  50.8 1.4 %collective-permute-start.14 = (bf16[2,8,2,16,256]{4,3,2,1,0:T(8,128)(2,1)S(1)}, bf16[2,8,2,16,256]{4,3,2,1,0:T(8,128)(2,1)S(1)}, u32[]{:S(2)}, u32[]{:S(2)}) collective-permute-start(bf16[2,8,2,16,256]{4,3,2,1,0:T(8,128)(2,1)S(1)} %pad_maximum_fusion.4), channel_id=1, source_target_pairs={{0,4},{2,6},{4,0},{6,2},{8,12},{10,14},{12,8},{14,10},{16,20},{18,... | collective-permute-start | bytes 786440 | tf_op jit(solution)/shard_map/ppermute | solution.py:127
  52.2 0.5 collective-permute-start.18
  52.9 1.0 collective-permute-done.9
  54.0 0.7 pad_maximum_fusion.2
  54.7 1.7 %collective-permute-start.11 = (bf16[2,8,2,16,256]{4,3,2,1,0:T(8,128)(2,1)}, bf16[2,8,2,16,256]{4,3,2,1,0:T(8,128)(2,1)}, u32[]{:S(2)}, u32[]{:S(2)}) collective-permute-start(bf16[2,8,2,16,256]{4,3,2,1,0:T(8,128)(2,1)} %pad_maximum_fusion.2), channel_id=1, source_target_pairs={{0,16},{2,18},{4,20},{6,22},{8,24},{10,26},{12,28},{14,30},{16,0},... | collective-permute-start | bytes 786440 | tf_op jit(solution)/shard_map/ppermute | solution.py:127
  56.4 1.4 %collective-permute-done.14 = bf16[2,8,2,16,256]{4,3,2,1,0:T(8,128)(2,1)S(1)} collective-permute-done((bf16[2,8,2,16,256]{4,3,2,1,0:T(8,128)(2,1)S(1)}, bf16[2,8,2,16,256]{4,3,2,1,0:T(8,128)(2,1)S(1)}, u32[]{:S(2)}, u32[]{:S(2)}) %collective-permute-start.14) | collective-permute-done | bytes 262176 | tf_op jit(solution)/shard_map/ppermute | solution.py:127
  57.9 0.7 fusion.1.refs_2_.refs_4_
  58.6 0.6 collective-permute-start.19
  59.2 0.6 collective-permute-done.15.refs_1_
  59.8 5.6 %cross_spectra.4 = bf16[16,32,4096]{2,1,0:T(8,128)(2,1)S(1)} custom-call(s32[1]{0:T(128)} %bitcast.place, bf16[4,8,2,16,256]{4,3,2,1,0:T(8,128)(2,1)S(1)} %pad_maximum_fusion.1.refs_0_, bf16[4,8,2,16,256]{4,3,2,1,0:T(8,128)(2,1)S(1)} %collective-permute-done.15.refs_1_, bf16[8,2,32,2048]{3,2,1,0:T(8,128)(2,1)S(1)} %fusion.1.refs_2_.refs_4_), custom_call_target="tpu_custom_call" | custom-call | flops 67108864 | bytes 1048576 | tf_op jit(solution)/shard_map/jit(cross_spectra)/pallas_call | solution.py:98
  65.4 1.2 %collective-permute-done.11 = bf16[2,8,2,16,256]{4,3,2,1,0:T(8,128)(2,1)} collective-permute-done((bf16[2,8,2,16,256]{4,3,2,1,0:T(8,128)(2,1)}, bf16[2,8,2,16,256]{4,3,2,1,0:T(8,128)(2,1)}, u32[]{:S(2)}, u32[]{:S(2)}) %collective-permute-start.11) | collective-permute-done | bytes 262176 | tf_op jit(solution)/shard_map/ppermute | solution.py:127
  66.7 1.2 %fusion.6 = (bf16[1,8,2,16,256]{4,3,2,1,0:T(8,128)(2,1)S(1)}, bf16[1,8,2,16,256]{4,3,2,1,0:T(8,128)(2,1)S(1)}) fusion(bf16[2,8,2,16,256]{4,3,2,1,0:T(8,128)(2,1)} %collective-permute-done.11, pred[]{:T(512)S(6)} %eq.31, bf16[8,2,16,256]{3,2,1,0:T(8,128)(2,1)S(1)} %copy-done.9, bf16[8,2,16,512]{3,2,1,0:T(8,128)(2,1)S(1)} %copy-done.7, s32[]{:T(128)S(6)} %mul.139, ...), kind=kLoop, calls=%fused_computation.32 | loop fusion | flops 262144 | bytes 1048588 | tf_op jit(solution)/shard_map/broadcast_in_dim | solution.py:226
  67.9 1.0 collective-permute-start.17
  69.0 2.3 %convolution_convert_fusion.1 = bf16[512,512]{1,0:T(8,128)(2,1)S(1)} fusion(bf16[512,4096]{1,0:T(8,128)(2,1)S(1)} %bitcast.61, bf16[4096,512]{1,0:T(8,128)(2,1)S(1)} %copy-done.12), kind=kOutput, calls=%fused_computation.7 | convolution fusion | flops 2147745792 | bytes 8912896 | tf_op jit(solution)/shard_map/dot_general | solution.py:241
  71.3 1.7 %collective-permute-start.24 = (bf16[512,512]{1,0:T(8,128)(2,1)S(1)}, bf16[512,512]{1,0:T(8,128)(2,1)S(1)}, u32[]{:S(2)}, u32[]{:S(2)}) collective-permute-start(bf16[512,512]{1,0:T(8,128)(2,1)S(1)} %convolution_convert_fusion.1), channel_id=1, source_target_pairs={{0,1},{1,0},{2,3},{3,2},{4,5},{5,4},{6,7},{7,6},{8,9},{9,8},{10,11... | collective-permute-start | bytes 1572872 | tf_op jit(solution)/shard_map/ppermute | solution.py:265
  73.3 2.0 %collective-permute-start.25 = (bf16[2,8,2,16,256]{4,3,2,1,0:T(8,128)(2,1)S(1)}, bf16[2,8,2,16,256]{4,3,2,1,0:T(8,128)(2,1)S(1)}, u32[]{:S(2)}, u32[]{:S(2)}) collective-permute-start(bf16[2,8,2,16,256]{4,3,2,1,0:T(8,128)(2,1)S(1)} %pad_maximum_fusion.7.refs_0_), channel_id=1, source_target_pairs={{0,8},{2,10},{4,12},{6,14},{8,0},{10,2},{12,4},{14,6},{16,24},{18,... | collective-permute-start | bytes 786440 | tf_op jit(solution)/shard_map/ppermute | solution.py:127
  75.4 1.1 %collective-permute-start.21 = (bf16[2,8,2,16,256]{4,3,2,1,0:T(8,128)(2,1)S(1)}, bf16[2,8,2,16,256]{4,3,2,1,0:T(8,128)(2,1)S(1)}, u32[]{:S(2)}, u32[]{:S(2)}) collective-permute-start(bf16[2,8,2,16,256]{4,3,2,1,0:T(8,128)(2,1)S(1)} %pad_maximum_fusion.5.refs_0_), channel_id=1, source_target_pairs={{0,4},{2,6},{4,0},{6,2},{8,12},{10,14},{12,8},{14,10},{16,20},{18,... | collective-permute-start | bytes 786440 | tf_op jit(solution)/shard_map/ppermute | solution.py:127
  76.4 6.5 %cross_spectra.5 = bf16[16,32,4096]{2,1,0:T(8,128)(2,1)S(1)} custom-call(s32[1]{0:T(128)} %bitcast.17.place, bf16[2,8,2,16,256]{4,3,2,1,0:T(8,128)(2,1)S(1)} %pad_maximum_fusion.6.refs_0_, bf16[2,8,2,16,256]{4,3,2,1,0:T(8,128)(2,1)} %collective-permute-done.18.refs_1_, bf16[2,8,2,16,256]{4,3,2,1,0:T(8,128)(2,1)S(1)} %collective-permute-done.19.refs_2_, ...), custom_call_target="tpu_custom_call" | custom-call | flops 67108864 | bytes 1048576 | tf_op jit(solution)/shard_map/jit(cross_spectra)/pallas_call | solution.py:98
  82.9 2.3 %convolution_convert_fusion = bf16[512,512]{1,0:T(8,128)(2,1)S(1)} fusion(bf16[512,4096]{1,0:T(8,128)(2,1)S(1)} %bitcast.64, bf16[4096,512]{1,0:T(8,128)(2,1)S(1)} %copy-done.12), kind=kOutput, calls=%fused_computation.6 | convolution fusion | flops 2147745792 | bytes 8912896 | tf_op jit(solution)/shard_map/dot_general | solution.py:241
  85.3 1.4 %collective-permute-start.28 = (bf16[512,512]{1,0:T(8,128)(2,1)S(1)}, bf16[512,512]{1,0:T(8,128)(2,1)S(1)}, u32[]{:S(2)}, u32[]{:S(2)}) collective-permute-start(bf16[512,512]{1,0:T(8,128)(2,1)S(1)} %convolution_convert_fusion), channel_id=1, source_target_pairs={{0,1},{1,0},{2,3},{3,2},{4,5},{5,4},{6,7},{7,6},{8,9},{9,8},{10,11... | collective-permute-start | bytes 1572872 | tf_op jit(solution)/shard_map/ppermute | solution.py:265
  87.2 0.9 collective-permute-done.23.refs_3_
  88.2 5.6 %cross_spectra.6 = bf16[16,32,4096]{2,1,0:T(8,128)(2,1)S(1)} custom-call(s32[1]{0:T(128)} %bitcast.place, bf16[2,8,2,16,256]{4,3,2,1,0:T(8,128)(2,1)S(1)} %pad_maximum_fusion.5.refs_0_, bf16[2,8,2,16,256]{4,3,2,1,0:T(8,128)(2,1)S(1)} %collective-permute-done.21.refs_1_, bf16[2,8,2,16,256]{4,3,2,1,0:T(8,128)(2,1)S(1)} %collective-permute-done.22.refs_2_, ...), custom_call_target="tpu_custom_call" | custom-call | flops 67108864 | bytes 1048576 | tf_op jit(solution)/shard_map/jit(cross_spectra)/pallas_call | solution.py:98
  93.8 5.6 %cross_spectra.7 = bf16[16,32,4096]{2,1,0:T(8,128)(2,1)S(1)} custom-call(s32[1]{0:T(128)} %bitcast.17.place, bf16[2,8,2,16,256]{4,3,2,1,0:T(8,128)(2,1)S(1)} %pad_maximum_fusion.7.refs_0_, bf16[2,8,2,16,256]{4,3,2,1,0:T(8,128)(2,1)S(1)} %collective-permute-done.25.refs_1_, bf16[2,8,2,16,256]{4,3,2,1,0:T(8,128)(2,1)S(1)} %collective-permute-done.26.refs_2_, ...), custom_call_target="tpu_custom_call" | custom-call | flops 67108864 | bytes 1048576 | tf_op jit(solution)/shard_map/jit(cross_spectra)/pallas_call | solution.py:98
  99.3 2.3 %fusion.14 = f32[512,512]{1,0:T(8,128)S(1)} fusion(bf16[512,4096]{1,0:T(8,128)(2,1)S(1)} %bitcast.63, bf16[4096,512]{1,0:T(8,128)(2,1)S(1)} %copy-done.12), kind=kOutput, calls=%fused_computation.58 | convolution fusion | flops 2147483648 | bytes 9437184 | tf_op jit(solution)/shard_map/dot_general | solution.py:241
  101.7 2.3 %fusion.13 = f32[512,512]{1,0:T(8,128)S(1)} fusion(bf16[512,4096]{1,0:T(8,128)(2,1)S(1)} %bitcast.62, bf16[4096,512]{1,0:T(8,128)(2,1)S(1)} %copy-done.12), kind=kOutput, calls=%fused_computation.57 | convolution fusion | flops 2147483648 | bytes 9437184 | tf_op jit(solution)/shard_map/dot_general | solution.py:241
  104.3 1.5 %pad_maximum_fusion = f32[16,2,32,512]{3,2,1,0:T(8,128)} fusion(f32[16,1,32,512]{3,2,1,0:T(8,128)S(1)} %bitcast.70, f32[16,1,32,512]{3,2,1,0:T(8,128)S(1)} %bitcast.69), kind=kLoop, calls=%fused_computation.4 | loop fusion | flops 524288 | bytes 4194304 | tf_op jit(solution)/shard_map/stack | solution.py:278
  (79 shorter events, 5.1 us)
Async XLA Ops:
  0.0 4.2 %copy-start.11 = (s32[32]{0:T(128)S(1)}, s32[32]{0:T(128)}, u32[]{:S(2)}) copy-start(s32[32]{0:T(128)} %param.6) | copy-start | bytes 388
  0.0 4.8 %copy-start.10 = (s32[2]{0:T(128)S(1)}, s32[2]{0:T(128)}, u32[]{:S(2)}) copy-start(s32[2]{0:T(128)} %param.5) | copy-start | bytes 28
  2.5 8.4 %copy-start = (bf16[8,32,2,2048]{3,1,2,0:T(8,128)(2,1)}, bf16[8,32,2,2048]{3,1,2,0:T(8,128)(2,1)S(1)}, u32[]{:S(2)}) copy-start(bf16[8,32,2,2048]{3,1,2,0:T(8,128)(2,1)S(1)} %copy.9) | copy-start | bytes 6291460
  3.7 3.1 %collective-permute-start.1 = (bf16[8,2,32,1024]{3,2,1,0:T(8,128)(2,1)}, bf16[8,2,32,1024]{3,2,1,0:T(8,128)(2,1)S(1)}, u32[]{:S(2)}, u32[]{:S(2)}) collective-permute-start(bf16[8,2,32,1024]{3,2,1,0:T(8,128)(2,1)} %constant_dynamic-slice_fusion.8), channel_id=1, source_target_pairs={{0,2},{2,0},{4,6},{6,4},{8,10},{10,8},{12,14},{14,12},{16,18},{18,... | collective-permute-start | bytes 3145736 | tf_op jit(solution)/shard_map/ppermute | solution.py:127
  4.7 2.1 %collective-permute-start = (f32[8,32]{1,0:T(8,128)S(1)}, f32[8,32]{1,0:T(8,128)S(1)}, u32[]{:S(2)}, u32[]{:S(2)}) collective-permute-start(f32[8,32]{1,0:T(8,128)S(1)} %rsqrt_multiply_fusion), channel_id=1, source_target_pairs={{0,2},{2,0},{4,6},{6,4},{8,10},{10,8},{12,14},{14,12},{16,18},{18,... | collective-permute-start | bytes 3080 | tf_op jit(solution)/shard_map/ppermute | solution.py:127
  10.9 33.9 %copy-start.3 = (bf16[8,2,32,512]{3,2,1,0:T(8,128)(2,1)S(1)}, bf16[8,2,32,512]{3,2,1,0:T(8,128)(2,1)}, u32[]{:S(2)}) copy-start(bf16[8,2,32,512]{3,2,1,0:T(8,128)(2,1)} %get-tuple-element.112) | copy-start | bytes 1572868
  10.9 36.3 %copy-start.2 = (bf16[8,2,32,512]{3,2,1,0:T(8,128)(2,1)S(1)}, bf16[8,2,32,512]{3,2,1,0:T(8,128)(2,1)}, u32[]{:S(2)}) copy-start(bf16[8,2,32,512]{3,2,1,0:T(8,128)(2,1)} %get-tuple-element.107) | copy-start | bytes 1572868
  11.4 9.5 %collective-permute-start.2 = (bf16[8,2,16,512]{3,2,1,0:T(8,128)(2,1)S(1)}, bf16[8,2,16,512]{3,2,1,0:T(8,128)(2,1)S(1)}, u32[]{:S(2)}, u32[]{:S(2)}) collective-permute-start(bf16[8,2,16,512]{3,2,1,0:T(8,128)(2,1)S(1)} %get-tuple-element.62), channel_id=1, source_target_pairs={{0,4},{2,6},{4,0},{6,2},{8,12},{10,14},{12,8},{14,10},{16,20},{18,... | collective-permute-start | bytes 786440 | tf_op jit(solution)/shard_map/ppermute | solution.py:127
  14.4 8.0 %collective-permute-start.3 = (bf16[8,2,16,512]{3,2,1,0:T(8,128)(2,1)S(1)}, bf16[8,2,16,512]{3,2,1,0:T(8,128)(2,1)S(1)}, u32[]{:S(2)}, u32[]{:S(2)}) collective-permute-start(bf16[8,2,16,512]{3,2,1,0:T(8,128)(2,1)S(1)} %get-tuple-element.63), channel_id=1, source_target_pairs={{0,8},{2,10},{4,12},{6,14},{8,0},{10,2},{12,4},{14,6},{16,24},{18,... | collective-permute-start | bytes 786440 | tf_op jit(solution)/shard_map/ppermute | solution.py:127
  23.6 5.0 %collective-permute-start.4 = (bf16[8,2,16,256]{3,2,1,0:T(8,128)(2,1)S(1)}, bf16[8,2,16,256]{3,2,1,0:T(8,128)(2,1)S(1)}, u32[]{:S(2)}, u32[]{:S(2)}) collective-permute-start(bf16[8,2,16,256]{3,2,1,0:T(8,128)(2,1)S(1)} %constant_dynamic-slice_fusion.3), channel_id=1, source_target_pairs={{0,8},{2,10},{4,12},{6,14},{8,0},{10,2},{12,4},{14,6},{16,24},{18,... | collective-permute-start | bytes 393224 | tf_op jit(solution)/shard_map/ppermute | solution.py:127
  26.3 31.7 %copy-start.1 = (bf16[8,32,2,2048]{3,1,2,0:T(8,128)(2,1)S(1)}, bf16[8,32,2,2048]{3,1,2,0:T(8,128)(2,1)}, u32[]{:S(2)}) copy-start(bf16[8,32,2,2048]{3,1,2,0:T(8,128)(2,1)} %copy-done) | copy-start | bytes 6291460
  26.4 5.0 %collective-permute-start.5 = (bf16[8,2,16,256]{3,2,1,0:T(8,128)(2,1)S(1)}, bf16[8,2,16,256]{3,2,1,0:T(8,128)(2,1)S(1)}, u32[]{:S(2)}, u32[]{:S(2)}) collective-permute-start(bf16[8,2,16,256]{3,2,1,0:T(8,128)(2,1)S(1)} %constant_dynamic-slice_fusion.2), channel_id=1, source_target_pairs={{0,4},{2,6},{4,0},{6,2},{8,12},{10,14},{12,8},{14,10},{16,20},{18,... | collective-permute-start | bytes 393224 | tf_op jit(solution)/shard_map/ppermute | solution.py:127
  31.6 12.3 %collective-permute-start.10 = (bf16[2,8,2,16,256]{4,3,2,1,0:T(8,128)(2,1)S(1)}, bf16[2,8,2,16,256]{4,3,2,1,0:T(8,128)(2,1)S(1)}, u32[]{:S(2)}, u32[]{:S(2)}) collective-permute-start(bf16[2,8,2,16,256]{4,3,2,1,0:T(8,128)(2,1)S(1)} %pad_maximum_fusion.3), channel_id=1, source_target_pairs={{0,16},{2,18},{4,20},{6,22},{8,24},{10,26},{12,28},{14,30},{16,0},... | collective-permute-start | bytes 786440 | tf_op jit(solution)/shard_map/ppermute | solution.py:127
  34.3 10.6 %collective-permute-start.6 = (bf16[8,2,16,512]{3,2,1,0:T(8,128)(2,1)S(1)}, bf16[8,2,16,512]{3,2,1,0:T(8,128)(2,1)S(1)}, u32[]{:S(2)}, u32[]{:S(2)}) collective-permute-start(bf16[8,2,16,512]{3,2,1,0:T(8,128)(2,1)S(1)} %get-tuple-element.77), channel_id=1, source_target_pairs={{0,4},{2,6},{4,0},{6,2},{8,12},{10,14},{12,8},{14,10},{16,20},{18,... | collective-permute-start | bytes 786440 | tf_op jit(solution)/shard_map/ppermute | solution.py:127
  34.8 12.4 %collective-permute-start.8 = (bf16[8,2,16,512]{3,2,1,0:T(8,128)(2,1)S(1)}, bf16[8,2,16,512]{3,2,1,0:T(8,128)(2,1)S(1)}, u32[]{:S(2)}, u32[]{:S(2)}) collective-permute-start(bf16[8,2,16,512]{3,2,1,0:T(8,128)(2,1)S(1)} %get-tuple-element.81), channel_id=1, source_target_pairs={{0,8},{2,10},{4,12},{6,14},{8,0},{10,2},{12,4},{14,6},{16,24},{18,... | collective-permute-start | bytes 786440 | tf_op jit(solution)/shard_map/ppermute | solution.py:127
  44.2 5.6 %collective-permute-start.13 = (bf16[1,8,2,16,256]{4,3,2,1,0:T(8,128)(2,1)S(1)}, bf16[1,8,2,16,256]{4,3,2,1,0:T(8,128)(2,1)S(1)}, u32[]{:S(2)}, u32[]{:S(2)}) collective-permute-start(bf16[1,8,2,16,256]{4,3,2,1,0:T(8,128)(2,1)S(1)} %get-tuple-element.119), channel_id=1, source_target_pairs={{0,4},{2,6},{4,0},{6,2},{8,12},{10,14},{12,8},{14,10},{16,20},{18,... | collective-permute-start | bytes 393224 | tf_op jit(solution)/shard_map/ppermute | solution.py:127
  44.8 6.0 %collective-permute-start.12 = (bf16[1,8,2,16,256]{4,3,2,1,0:T(8,128)(2,1)S(1)}, bf16[1,8,2,16,256]{4,3,2,1,0:T(8,128)(2,1)S(1)}, u32[]{:S(2)}, u32[]{:S(2)}) collective-permute-start(bf16[1,8,2,16,256]{4,3,2,1,0:T(8,128)(2,1)S(1)} %get-tuple-element.120), channel_id=1, source_target_pairs={{0,8},{2,10},{4,12},{6,14},{8,0},{10,2},{12,4},{14,6},{16,24},{18,... | collective-permute-start | bytes 393224 | tf_op jit(solution)/shard_map/ppermute | solution.py:127
  45.0 11.5 %copy-start.4 = (bf16[8,2,16,512]{3,2,1,0:T(8,128)(2,1)}, bf16[8,2,16,512]{3,2,1,0:T(8,128)(2,1)S(1)}, u32[]{:S(2)}) copy-start(bf16[8,2,16,512]{3,2,1,0:T(8,128)(2,1)S(1)} %dynamic-slice_select_fusion.3) | copy-start | bytes 786436
  45.1 7.7 %collective-permute-start.7 = (bf16[8,2,16,256]{3,2,1,0:T(8,128)(2,1)S(1)}, bf16[8,2,16,256]{3,2,1,0:T(8,128)(2,1)S(1)}, u32[]{:S(2)}, u32[]{:S(2)}) collective-permute-start(bf16[8,2,16,256]{3,2,1,0:T(8,128)(2,1)S(1)} %constant_dynamic-slice_fusion), channel_id=1, source_target_pairs={{0,8},{2,10},{4,12},{6,14},{8,0},{10,2},{12,4},{14,6},{16,24},{18,... | collective-permute-start | bytes 393224 | tf_op jit(solution)/shard_map/ppermute | solution.py:127
  47.3 9.1 %copy-start.6 = (bf16[8,2,16,512]{3,2,1,0:T(8,128)(2,1)}, bf16[8,2,16,512]{3,2,1,0:T(8,128)(2,1)S(1)}, u32[]{:S(2)}) copy-start(bf16[8,2,16,512]{3,2,1,0:T(8,128)(2,1)S(1)} %dynamic-slice_select_fusion) | copy-start | bytes 786436
  47.4 6.4 %collective-permute-start.9 = (bf16[8,2,16,256]{3,2,1,0:T(8,128)(2,1)S(1)}, bf16[8,2,16,256]{3,2,1,0:T(8,128)(2,1)S(1)}, u32[]{:S(2)}, u32[]{:S(2)}) collective-permute-start(bf16[8,2,16,256]{3,2,1,0:T(8,128)(2,1)S(1)} %constant_dynamic-slice_fusion.6), channel_id=1, source_target_pairs={{0,4},{2,6},{4,0},{6,2},{8,12},{10,14},{12,8},{14,10},{16,20},{18,... | collective-permute-start | bytes 393224 | tf_op jit(solution)/shard_map/ppermute | solution.py:127
  50.8 7.0 %collective-permute-start.14 = (bf16[2,8,2,16,256]{4,3,2,1,0:T(8,128)(2,1)S(1)}, bf16[2,8,2,16,256]{4,3,2,1,0:T(8,128)(2,1)S(1)}, u32[]{:S(2)}, u32[]{:S(2)}) collective-permute-start(bf16[2,8,2,16,256]{4,3,2,1,0:T(8,128)(2,1)S(1)} %pad_maximum_fusion.4), channel_id=1, source_target_pairs={{0,4},{2,6},{4,0},{6,2},{8,12},{10,14},{12,8},{14,10},{16,20},{18,... | collective-permute-start | bytes 786440 | tf_op jit(solution)/shard_map/ppermute | solution.py:127
  52.2 13.2 %collective-permute-start.18 = (bf16[2,8,2,16,256]{4,3,2,1,0:T(8,128)(2,1)S(1)}, bf16[2,8,2,16,256]{4,3,2,1,0:T(8,128)(2,1)}, u32[]{:S(2)}, u32[]{:S(2)}) collective-permute-start(bf16[2,8,2,16,256]{4,3,2,1,0:T(8,128)(2,1)S(1)} %pad_maximum_fusion.6.refs_0_), channel_id=1, source_target_pairs={{0,8},{2,10},{4,12},{6,14},{8,0},{10,2},{12,4},{14,6},{16,24},{18,... | collective-permute-start | bytes 786440 | tf_op jit(solution)/shard_map/ppermute | solution.py:127
  53.9 2.6 %copy-start.8 = (bf16[8,2,16,256]{3,2,1,0:T(8,128)(2,1)}, bf16[8,2,16,256]{3,2,1,0:T(8,128)(2,1)S(1)}, u32[]{:S(2)}) copy-start(bf16[8,2,16,256]{3,2,1,0:T(8,128)(2,1)S(1)} %collective-permute-done.9) | copy-start | bytes 393220
  54.7 11.9 %collective-permute-start.11 = (bf16[2,8,2,16,256]{4,3,2,1,0:T(8,128)(2,1)}, bf16[2,8,2,16,256]{4,3,2,1,0:T(8,128)(2,1)}, u32[]{:S(2)}, u32[]{:S(2)}) collective-permute-start(bf16[2,8,2,16,256]{4,3,2,1,0:T(8,128)(2,1)} %pad_maximum_fusion.2), channel_id=1, source_target_pairs={{0,16},{2,18},{4,20},{6,22},{8,24},{10,26},{12,28},{14,30},{16,0},... | collective-permute-start | bytes 786440 | tf_op jit(solution)/shard_map/ppermute | solution.py:127
  57.9 2.0 %collective-permute-start.15 = (bf16[4,8,2,16,256]{4,3,2,1,0:T(8,128)(2,1)S(1)}, bf16[4,8,2,16,256]{4,3,2,1,0:T(8,128)(2,1)S(1)}, u32[]{:S(2)}, u32[]{:S(2)}) collective-permute-start(bf16[4,8,2,16,256]{4,3,2,1,0:T(8,128)(2,1)S(1)} %pad_maximum_fusion.1.refs_0_), channel_id=1, source_target_pairs={{0,2},{2,0},{4,6},{6,4},{8,10},{10,8},{12,14},{14,12},{16,18},{18,... | collective-permute-start | bytes 1572872 | tf_op jit(solution)/shard_map/ppermute | solution.py:127
  58.6 8.0 %copy-start.5 = (bf16[8,2,16,512]{3,2,1,0:T(8,128)(2,1)S(1)}, bf16[8,2,16,512]{3,2,1,0:T(8,128)(2,1)}, u32[]{:S(2)}) copy-start(bf16[8,2,16,512]{3,2,1,0:T(8,128)(2,1)} %copy-done.4) | copy-start | bytes 786436
  58.6 8.0 %copy-start.7 = (bf16[8,2,16,512]{3,2,1,0:T(8,128)(2,1)S(1)}, bf16[8,2,16,512]{3,2,1,0:T(8,128)(2,1)}, u32[]{:S(2)}) copy-start(bf16[8,2,16,512]{3,2,1,0:T(8,128)(2,1)} %copy-done.6) | copy-start | bytes 786436
  58.6 8.0 %copy-start.9 = (bf16[8,2,16,256]{3,2,1,0:T(8,128)(2,1)S(1)}, bf16[8,2,16,256]{3,2,1,0:T(8,128)(2,1)}, u32[]{:S(2)}) copy-start(bf16[8,2,16,256]{3,2,1,0:T(8,128)(2,1)} %copy-done.8) | copy-start | bytes 393220
  58.6 16.7 %collective-permute-start.19 = (bf16[2,8,2,16,256]{4,3,2,1,0:T(8,128)(2,1)S(1)}, bf16[2,8,2,16,256]{4,3,2,1,0:T(8,128)(2,1)S(1)}, u32[]{:S(2)}, u32[]{:S(2)}) collective-permute-start(bf16[2,8,2,16,256]{4,3,2,1,0:T(8,128)(2,1)S(1)} %pad_maximum_fusion.6.refs_0_), channel_id=1, source_target_pairs={{0,2},{2,0},{4,6},{6,4},{8,10},{10,8},{12,14},{14,12},{16,18},{18,... | collective-permute-start | bytes 786440 | tf_op jit(solution)/shard_map/ppermute | solution.py:127
  59.8 9.1 %copy-start.12 = (bf16[4096,512]{1,0:T(8,128)(2,1)S(1)}, bf16[4096,512]{1,0:T(8,128)(2,1)}, u32[]{:S(2)}) copy-start(bf16[4096,512]{1,0:T(8,128)(2,1)} %constant.106.clone) | copy-start | bytes 12582916
  67.9 5.1 %collective-permute-start.16 = (bf16[1,8,2,16,256]{4,3,2,1,0:T(8,128)(2,1)S(1)}, bf16[1,8,2,16,256]{4,3,2,1,0:T(8,128)(2,1)S(1)}, u32[]{:S(2)}, u32[]{:S(2)}) collective-permute-start(bf16[1,8,2,16,256]{4,3,2,1,0:T(8,128)(2,1)S(1)} %get-tuple-element.88), channel_id=1, source_target_pairs={{0,8},{2,10},{4,12},{6,14},{8,0},{10,2},{12,4},{14,6},{16,24},{18,... | collective-permute-start | bytes 393224 | tf_op jit(solution)/shard_map/ppermute | solution.py:127
  67.9 5.0 %collective-permute-start.17 = (bf16[1,8,2,16,256]{4,3,2,1,0:T(8,128)(2,1)S(1)}, bf16[1,8,2,16,256]{4,3,2,1,0:T(8,128)(2,1)S(1)}, u32[]{:S(2)}, u32[]{:S(2)}) collective-permute-start(bf16[1,8,2,16,256]{4,3,2,1,0:T(8,128)(2,1)S(1)} %get-tuple-element.89), channel_id=1, source_target_pairs={{0,4},{2,6},{4,0},{6,2},{8,12},{10,14},{12,8},{14,10},{16,20},{18,... | collective-permute-start | bytes 393224 | tf_op jit(solution)/shard_map/ppermute | solution.py:127
  69.0 7.5 %collective-permute-start.20 = (bf16[2,8,2,16,256]{4,3,2,1,0:T(8,128)(2,1)}, bf16[2,8,2,16,256]{4,3,2,1,0:T(8,128)(2,1)S(1)}, u32[]{:S(2)}, u32[]{:S(2)}) collective-permute-start(bf16[2,8,2,16,256]{4,3,2,1,0:T(8,128)(2,1)} %collective-permute-done.18.refs_1_), channel_id=1, source_target_pairs={{0,2},{2,0},{4,6},{6,4},{8,10},{10,8},{12,14},{14,12},{16,18},{18,... | collective-permute-start | bytes 786440 | tf_op jit(solution)/shard_map/ppermute | solution.py:127
  71.3 22.4 %collective-permute-start.24 = (bf16[512,512]{1,0:T(8,128)(2,1)S(1)}, bf16[512,512]{1,0:T(8,128)(2,1)S(1)}, u32[]{:S(2)}, u32[]{:S(2)}) collective-permute-start(bf16[512,512]{1,0:T(8,128)(2,1)S(1)} %convolution_convert_fusion.1), channel_id=1, source_target_pairs={{0,1},{1,0},{2,3},{3,2},{4,5},{5,4},{6,7},{7,6},{8,9},{9,8},{10,11... | collective-permute-start | bytes 1572872 | tf_op jit(solution)/shard_map/ppermute | solution.py:265
  73.0 14.1 %collective-permute-start.22 = (bf16[2,8,2,16,256]{4,3,2,1,0:T(8,128)(2,1)S(1)}, bf16[2,8,2,16,256]{4,3,2,1,0:T(8,128)(2,1)S(1)}, u32[]{:S(2)}, u32[]{:S(2)}) collective-permute-start(bf16[2,8,2,16,256]{4,3,2,1,0:T(8,128)(2,1)S(1)} %pad_maximum_fusion.5.refs_0_), channel_id=1, source_target_pairs={{0,2},{2,0},{4,6},{6,4},{8,10},{10,8},{12,14},{14,12},{16,18},{18,... | collective-permute-start | bytes 786440 | tf_op jit(solution)/shard_map/ppermute | solution.py:127
  73.3 13.3 %collective-permute-start.25 = (bf16[2,8,2,16,256]{4,3,2,1,0:T(8,128)(2,1)S(1)}, bf16[2,8,2,16,256]{4,3,2,1,0:T(8,128)(2,1)S(1)}, u32[]{:S(2)}, u32[]{:S(2)}) collective-permute-start(bf16[2,8,2,16,256]{4,3,2,1,0:T(8,128)(2,1)S(1)} %pad_maximum_fusion.7.refs_0_), channel_id=1, source_target_pairs={{0,8},{2,10},{4,12},{6,14},{8,0},{10,2},{12,4},{14,6},{16,24},{18,... | collective-permute-start | bytes 786440 | tf_op jit(solution)/shard_map/ppermute | solution.py:127
  75.4 11.3 %collective-permute-start.21 = (bf16[2,8,2,16,256]{4,3,2,1,0:T(8,128)(2,1)S(1)}, bf16[2,8,2,16,256]{4,3,2,1,0:T(8,128)(2,1)S(1)}, u32[]{:S(2)}, u32[]{:S(2)}) collective-permute-start(bf16[2,8,2,16,256]{4,3,2,1,0:T(8,128)(2,1)S(1)} %pad_maximum_fusion.5.refs_0_), channel_id=1, source_target_pairs={{0,4},{2,6},{4,0},{6,2},{8,12},{10,14},{12,8},{14,10},{16,20},{18,... | collective-permute-start | bytes 786440 | tf_op jit(solution)/shard_map/ppermute | solution.py:127
  85.3 14.1 %collective-permute-start.28 = (bf16[512,512]{1,0:T(8,128)(2,1)S(1)}, bf16[512,512]{1,0:T(8,128)(2,1)S(1)}, u32[]{:S(2)}, u32[]{:S(2)}) collective-permute-start(bf16[512,512]{1,0:T(8,128)(2,1)S(1)} %convolution_convert_fusion), channel_id=1, source_target_pairs={{0,1},{1,0},{2,3},{3,2},{4,5},{5,4},{6,7},{7,6},{8,9},{9,8},{10,11... | collective-permute-start | bytes 1572872 | tf_op jit(solution)/shard_map/ppermute | solution.py:265
  86.6 1.5 %collective-permute-start.23 = (bf16[2,8,2,16,256]{4,3,2,1,0:T(8,128)(2,1)S(1)}, bf16[2,8,2,16,256]{4,3,2,1,0:T(8,128)(2,1)S(1)}, u32[]{:S(2)}, u32[]{:S(2)}) collective-permute-start(bf16[2,8,2,16,256]{4,3,2,1,0:T(8,128)(2,1)S(1)} %collective-permute-done.21.refs_1_), channel_id=1, source_target_pairs={{0,2},{2,0},{4,6},{6,4},{8,10},{10,8},{12,14},{14,12},{16,18},{18,... | collective-permute-start | bytes 786440 | tf_op jit(solution)/shard_map/ppermute | solution.py:127
  86.6 7.1 %collective-permute-start.26 = (bf16[2,8,2,16,256]{4,3,2,1,0:T(8,128)(2,1)S(1)}, bf16[2,8,2,16,256]{4,3,2,1,0:T(8,128)(2,1)S(1)}, u32[]{:S(2)}, u32[]{:S(2)}) collective-permute-start(bf16[2,8,2,16,256]{4,3,2,1,0:T(8,128)(2,1)S(1)} %pad_maximum_fusion.7.refs_0_), channel_id=1, source_target_pairs={{0,2},{2,0},{4,6},{6,4},{8,10},{10,8},{12,14},{14,12},{16,18},{18,... | collective-permute-start | bytes 786440 | tf_op jit(solution)/shard_map/ppermute | solution.py:127
  87.1 6.6 %collective-permute-start.27 = (bf16[2,8,2,16,256]{4,3,2,1,0:T(8,128)(2,1)S(1)}, bf16[2,8,2,16,256]{4,3,2,1,0:T(8,128)(2,1)S(1)}, u32[]{:S(2)}, u32[]{:S(2)}) collective-permute-start(bf16[2,8,2,16,256]{4,3,2,1,0:T(8,128)(2,1)S(1)} %collective-permute-done.25.refs_1_), channel_id=1, source_target_pairs={{0,2},{2,0},{4,6},{6,4},{8,10},{10,8},{12,14},{14,12},{16,18},{18,... | collective-permute-start | bytes 786440 | tf_op jit(solution)/shard_map/ppermute | solution.py:127
